TPU v7x, 256 devices: a whole 4x4x8 slice. The times are simulated.
256 devices in a mesh: cube: 4 (over y_hi, core), row: 8 (over x, y_lo), col: 8 (over z).
Axes of the slice: x: 4, y: 4 (y_hi: 2, y_lo: 2; y = y_hi * 2 + y_lo), z: 8, core: 2. Of those that a mesh axis runs over, the one named last changes fastest.
Arguments:
- child_fronts: bfloat16 [4, 32, 128, 8, 8, 128], P(None, ('cube', 'row'), None, None, 'col')
- root_front: bfloat16 [4, 32, 128, 16, 8, 128], P(None, ('cube', 'row'), None, None, 'col')
- child_pivots: float32 [2, 10, 128, 128], replicated, as said below
- root_pivots: float32 [4, 128, 128], replicated, as said below
- child_maps: int32 [2, 54], replicated, may hold values from 10 to 127, as said below
Outputs:
- child_factor: bfloat16 [4, 32, 128, 1280], P(None, ('cube', 'row'))
- root_factor: bfloat16 [4, 32, 128, 512], P(None, ('cube', 'row'))
- root_rest: bfloat16 [4, 32, 128, 16, 8, 128], P(None, ('cube', 'row'), None, None, 'col')
Inputs may be any that keep to these rules, and one draw needn't show every extreme that they name: `child_maps`: entry [c, a] is the root tile row that receives update tile row a of child c; each row of the list strictly increases, and entry [c, a] is congruent to a + 10 modulo 32. `child_pivots`: each block is zero below its diagonal. `root_pivots`: each block is zero below its diagonal.
All inputs are finite; a program needn't handle non-finite values.
Results may differ from a plain program's by a relative error of at most 0.0034.
Values may be sent and summed in bfloat16 or wider, within the bound.
A program may use at most 64 MiB of HBM per device.

v0:
```python
import jax
import jax.numpy as jnp
from jax import lax
from jax.sharding import PartitionSpec as P


def from_root(block, axis, holder):
    block = jnp.where(lax.axis_index(axis) == holder, block, jnp.zeros_like(block))
    return lax.psum(block, axis)


def from_partner(value, axis, distance):
    mask = 2**distance
    pairs = [(source, source ^ mask) for source in range(lax.axis_size(axis))]
    return lax.ppermute(value, axis, pairs)


def share_down(payload, panel_step):
    return from_root(payload, "col", panel_step % lax.axis_size("col"))


def child_side(payload, panel_step):
    per_row = lax.axis_size("row")
    spread = from_root(payload, "row", panel_step % per_row)
    partner = from_partner(spread, "cube", 0)
    owns_half = lax.axis_index("cube") % 2 == panel_step // per_row % 2
    return jnp.where(owns_half, spread, partner)


def root_columns(payload, panel_step):
    per_row = lax.axis_size("row")
    owner_index = panel_step % (lax.axis_size("cube") * per_row)
    return from_root(payload, ("cube", "row"), owner_index)


def eliminate_local(working, pivots, period, offset, send_side):
    panel_count = pivots.shape[0]
    tile_size = pivots.shape[1]
    columns_each = lax.axis_size("col")
    column_index = lax.axis_index("col")
    row_globals = jnp.arange(working.shape[0] // tile_size) * period + offset
    col_globals = jnp.arange(working.shape[1] // tile_size) * columns_each + column_index
    factor_panels = jnp.zeros((working.shape[0], panel_count * tile_size), jnp.bfloat16)

    def slices(matrix, panel_step):
        column = lax.dynamic_slice_in_dim(
            matrix, panel_step // columns_each * tile_size, tile_size, 1
        )
        across = lax.dynamic_slice_in_dim(matrix, panel_step // period * tile_size, tile_size, 0)
        return (column, across)

    def prepare(column, across, panel_step):
        pivot = lax.dynamic_index_in_dim(pivots, panel_step, 0, keepdims=False)
        down_part = jnp.dot(
            column, pivot, precision=lax.Precision.HIGHEST, preferred_element_type=jnp.float32
        )
        side_part = lax.dot_general(
            across,
            pivot,
            (((0,), (0,)), ((), ())),
            precision=lax.Precision.HIGHEST,
            preferred_element_type=jnp.float32,
        )
        row_keep = jnp.repeat(row_globals >= panel_step, tile_size)
        col_keep = jnp.repeat(col_globals >= panel_step, tile_size)
        down_part = jnp.where(row_keep[:, None], down_part, 0.0).astype(jnp.bfloat16)
        side_part = jnp.where(col_keep[:, None], side_part, 0.0).astype(jnp.bfloat16)
        return (down_part, side_part)

    def outer(left_part, right_part):
        return lax.dot_general(
            left_part, right_part, (((1,), (1,)), ((), ())), preferred_element_type=jnp.float32
        )

    def record(done, down_part, panel_step):
        return lax.dynamic_update_slice_in_dim(done, down_part, panel_step * tile_size, 1)

    def advance(panel_step, carried):
        matrix, done = carried
        column, across = slices(matrix, panel_step)
        down_part, side_part = prepare(column, across, panel_step)
        down_part = share_down(down_part, panel_step)
        side_part = send_side(side_part, panel_step)
        return (matrix - outer(down_part, side_part), record(done, down_part, panel_step))

    working, factor_panels = lax.fori_loop(0, panel_count, advance, (working, factor_panels))
    return (working, factor_panels)


def on_device(child_fronts, root_front, child_pivots, root_pivots, child_maps):
    tile_size = child_pivots.shape[-1]
    per_row = lax.axis_size("row")
    per_col = lax.axis_size("col")
    cube_index = lax.axis_index("cube")
    row_index = lax.axis_index("row")
    col_index = lax.axis_index("col")
    child_index = cube_index // 2
    half_index = cube_index % 2
    child_rows = child_fronts.shape[0] * tile_size
    child_cols = child_fronts.shape[3] * tile_size
    working = child_fronts.reshape(child_rows, child_cols).astype(jnp.float32)
    pivots = lax.dynamic_index_in_dim(child_pivots, child_index, 0, keepdims=False)
    working, child_panels = eliminate_local(
        working, pivots, 2 * per_row, half_index * per_row + row_index, child_side
    )
    first_tile = child_pivots.shape[1]
    update = working.astype(jnp.bfloat16)
    tile_pairs = update.reshape(-1, 2, tile_size, child_cols)
    kept_tiles = lax.dynamic_index_in_dim(tile_pairs, child_index, 1, keepdims=False)
    outgoing = lax.dynamic_index_in_dim(tile_pairs, 1 - child_index, 1, keepdims=False)
    incoming = from_partner(outgoing, "cube", 1)
    root_tiles = root_front.shape[0]
    root_cols = root_front.shape[3]
    row_classes = lax.axis_size("cube") * per_row
    kept_global = (
        (2 * jnp.arange(kept_tiles.shape[0]) + child_index) * (2 * per_row)
        + half_index * per_row
        + row_index
    )
    col_global = jnp.arange(child_cols // tile_size) * per_col + col_index

    def placed(tiles_in, source):
        row_table = lax.dynamic_index_in_dim(child_maps, source, 0, keepdims=False)
        table_length = row_table.shape[0]

        def lookup(global_tiles):
            position = global_tiles - first_tile
            matches = position[:, None] == jnp.arange(table_length)[None, :]
            target = jnp.sum(jnp.where(matches, row_table[None, :], 0), axis=1)
            return (jnp.any(matches, axis=1), target)

        row_live, row_dest = lookup(kept_global)
        col_live, col_dest = lookup(col_global)
        row_pick = (
            row_live[:, None]
            & (row_dest[:, None] // row_classes == jnp.arange(root_tiles)[None, :])
        ).astype(jnp.bfloat16)
        col_pick = (
            col_live[:, None] & (col_dest[:, None] // per_col == jnp.arange(root_cols)[None, :])
        ).astype(jnp.bfloat16)
        flattened = tiles_in.reshape(tiles_in.shape[0], -1)
        moved = lax.dot_general(
            row_pick, flattened, (((0,), (0,)), ((), ())), preferred_element_type=jnp.float32
        ).astype(jnp.bfloat16)
        moved = moved.reshape(root_tiles * tile_size, child_cols // tile_size, tile_size)
        spread = jnp.einsum("rsb,sv->rvb", moved, col_pick, preferred_element_type=jnp.float32)
        return spread.reshape(root_tiles * tile_size, root_cols * tile_size)

    root_matrix = root_front.reshape(root_tiles * tile_size, root_cols * tile_size).astype(
        jnp.float32
    )
    root_matrix = root_matrix + placed(kept_tiles, child_index) + placed(incoming, 1 - child_index)
    root_matrix, root_panels = eliminate_local(
        root_matrix, root_pivots, row_classes, cube_index * per_row + row_index, root_columns
    )
    child_factor = child_panels.reshape(child_fronts.shape[0], 1, tile_size, child_panels.shape[1])
    root_factor = root_panels.reshape(root_tiles, 1, tile_size, root_panels.shape[1])
    root_rest = root_matrix.astype(jnp.bfloat16).reshape(
        root_tiles, 1, tile_size, root_cols, 1, tile_size
    )
    return (child_factor, root_factor, root_rest)


def solution(mesh):
    placed = (
        P(None, ("cube", "row"), None, None, "col", None),
        P(None, ("cube", "row"), None, None, "col", None),
        P(),
        P(),
        P(),
    )
    return jax.shard_map(
        on_device,
        mesh=mesh,
        in_specs=placed,
        out_specs=(
            P(None, ("cube", "row"), None, None),
            P(None, ("cube", "row"), None, None),
            P(None, ("cube", "row"), None, None, "col", None),
        ),
        check_vma=False,
    )
```

profile of v0, /device:TPU:25, one launch (start us, length us, event | category | flops | bytes accessed | tf_op | source)
XLA Modules:
  0.0 2427.8 jit_solution(18343242720477282117)
XLA Ops:
  10.8 1584.9 %while.38 = (s32[]{:T(128)}, f32[512,1024]{1,0:T(8,128)S(1)}, bf16[512,1280]{1,0:T(8,128)(2,1)}, f32[10,128,128]{2,1,0:T(8,128)}, s32[]{:T(128)}, /*index=5*/s32...) while((s32[]{:T(128)}, f32[512,1024]{1,0:T(8,128)S(1)}, ...), condition=%wide.region_3.4_spmd.clone, body=%wide.region_0.3_spmd.clone.sunk | while | flops 437649472 | bytes 9835511 | solution.py:86
  13.7 76.2 %all-reduce.7.cloned.1.call-done = bf16[1024,128]{1,0:T(8,128)(2,1)} async-done(((bf16[1024,128]{1,0:T(8,128)(2,1)}), bf16[1024,128]{1,0:T(8,128)(2,1)}) %all-reduce.7.cloned.1.call-update) | async-done | bytes 262160 | tf_op jit(solution)/shard_map/while/body/eval_jaxpr/psum | solution.py:9
  97.1 68.5 %all-reduce.5.cloned.1.call-done = bf16[512,128]{1,0:T(8,128)(2,1)} async-done(((bf16[512,128]{1,0:T(8,128)(2,1)}), bf16[512,128]{1,0:T(8,128)(2,1)}) %all-reduce.5.cloned.1.call-update) | async-done | bytes 131088 | tf_op jit(solution)/shard_map/while/body/eval_jaxpr/psum | solution.py:9
  171.8 76.9 %all-reduce.7.cloned.1.call-done = bf16[1024,128]{1,0:T(8,128)(2,1)} async-done(((bf16[1024,128]{1,0:T(8,128)(2,1)}), bf16[1024,128]{1,0:T(8,128)(2,1)}) %all-reduce.7.cloned.1.call-update) | async-done | bytes 262160 | tf_op jit(solution)/shard_map/while/body/eval_jaxpr/psum | solution.py:9
  255.9 68.4 %all-reduce.5.cloned.1.call-done = bf16[512,128]{1,0:T(8,128)(2,1)} async-done(((bf16[512,128]{1,0:T(8,128)(2,1)}), bf16[512,128]{1,0:T(8,128)(2,1)}) %all-reduce.5.cloned.1.call-update) | async-done | bytes 131088 | tf_op jit(solution)/shard_map/while/body/eval_jaxpr/psum | solution.py:9
  330.4 76.6 %all-reduce.7.cloned.1.call-done = bf16[1024,128]{1,0:T(8,128)(2,1)} async-done(((bf16[1024,128]{1,0:T(8,128)(2,1)}), bf16[1024,128]{1,0:T(8,128)(2,1)}) %all-reduce.7.cloned.1.call-update) | async-done | bytes 262160 | tf_op jit(solution)/shard_map/while/body/eval_jaxpr/psum | solution.py:9
  414.2 68.4 %all-reduce.5.cloned.1.call-done = bf16[512,128]{1,0:T(8,128)(2,1)} async-done(((bf16[512,128]{1,0:T(8,128)(2,1)}), bf16[512,128]{1,0:T(8,128)(2,1)}) %all-reduce.5.cloned.1.call-update) | async-done | bytes 131088 | tf_op jit(solution)/shard_map/while/body/eval_jaxpr/psum | solution.py:9
  488.7 76.9 %all-reduce.7.cloned.1.call-done = bf16[1024,128]{1,0:T(8,128)(2,1)} async-done(((bf16[1024,128]{1,0:T(8,128)(2,1)}), bf16[1024,128]{1,0:T(8,128)(2,1)}) %all-reduce.7.cloned.1.call-update) | async-done | bytes 262160 | tf_op jit(solution)/shard_map/while/body/eval_jaxpr/psum | solution.py:9
  572.9 68.5 %all-reduce.5.cloned.1.call-done = bf16[512,128]{1,0:T(8,128)(2,1)} async-done(((bf16[512,128]{1,0:T(8,128)(2,1)}), bf16[512,128]{1,0:T(8,128)(2,1)}) %all-reduce.5.cloned.1.call-update) | async-done | bytes 131088 | tf_op jit(solution)/shard_map/while/body/eval_jaxpr/psum | solution.py:9
  647.5 76.9 %all-reduce.7.cloned.1.call-done = bf16[1024,128]{1,0:T(8,128)(2,1)} async-done(((bf16[1024,128]{1,0:T(8,128)(2,1)}), bf16[1024,128]{1,0:T(8,128)(2,1)}) %all-reduce.7.cloned.1.call-update) | async-done | bytes 262160 | tf_op jit(solution)/shard_map/while/body/eval_jaxpr/psum | solution.py:9
  806.2 76.9 %all-reduce.7.cloned.1.call-done = bf16[1024,128]{1,0:T(8,128)(2,1)} async-done(((bf16[1024,128]{1,0:T(8,128)(2,1)}), bf16[1024,128]{1,0:T(8,128)(2,1)}) %all-reduce.7.cloned.1.call-update) | async-done | bytes 262160 | tf_op jit(solution)/shard_map/while/body/eval_jaxpr/psum | solution.py:9
  890.3 68.4 %all-reduce.5.cloned.1.call-done = bf16[512,128]{1,0:T(8,128)(2,1)} async-done(((bf16[512,128]{1,0:T(8,128)(2,1)}), bf16[512,128]{1,0:T(8,128)(2,1)}) %all-reduce.5.cloned.1.call-update) | async-done | bytes 131088 | tf_op jit(solution)/shard_map/while/body/eval_jaxpr/psum | solution.py:9
  964.8 76.9 %all-reduce.7.cloned.1.call-done = bf16[1024,128]{1,0:T(8,128)(2,1)} async-done(((bf16[1024,128]{1,0:T(8,128)(2,1)}), bf16[1024,128]{1,0:T(8,128)(2,1)}) %all-reduce.7.cloned.1.call-update) | async-done | bytes 262160 | tf_op jit(solution)/shard_map/while/body/eval_jaxpr/psum | solution.py:9
  1048.9 68.4 %all-reduce.5.cloned.1.call-done = bf16[512,128]{1,0:T(8,128)(2,1)} async-done(((bf16[512,128]{1,0:T(8,128)(2,1)}), bf16[512,128]{1,0:T(8,128)(2,1)}) %all-reduce.5.cloned.1.call-update) | async-done | bytes 131088 | tf_op jit(solution)/shard_map/while/body/eval_jaxpr/psum | solution.py:9
  1123.4 76.6 %all-reduce.7.cloned.1.call-done = bf16[1024,128]{1,0:T(8,128)(2,1)} async-done(((bf16[1024,128]{1,0:T(8,128)(2,1)}), bf16[1024,128]{1,0:T(8,128)(2,1)}) %all-reduce.7.cloned.1.call-update) | async-done | bytes 262160 | tf_op jit(solution)/shard_map/while/body/eval_jaxpr/psum | solution.py:9
  1207.2 68.4 %all-reduce.5.cloned.1.call-done = bf16[512,128]{1,0:T(8,128)(2,1)} async-done(((bf16[512,128]{1,0:T(8,128)(2,1)}), bf16[512,128]{1,0:T(8,128)(2,1)}) %all-reduce.5.cloned.1.call-update) | async-done | bytes 131088 | tf_op jit(solution)/shard_map/while/body/eval_jaxpr/psum | solution.py:9
  1281.7 76.6 %all-reduce.7.cloned.1.call-done = bf16[1024,128]{1,0:T(8,128)(2,1)} async-done(((bf16[1024,128]{1,0:T(8,128)(2,1)}), bf16[1024,128]{1,0:T(8,128)(2,1)}) %all-reduce.7.cloned.1.call-update) | async-done | bytes 262160 | tf_op jit(solution)/shard_map/while/body/eval_jaxpr/psum | solution.py:9
  1365.6 68.4 %all-reduce.5.cloned.1.call-done = bf16[512,128]{1,0:T(8,128)(2,1)} async-done(((bf16[512,128]{1,0:T(8,128)(2,1)}), bf16[512,128]{1,0:T(8,128)(2,1)}) %all-reduce.5.cloned.1.call-update) | async-done | bytes 131088 | tf_op jit(solution)/shard_map/while/body/eval_jaxpr/psum | solution.py:9
  1440.1 76.9 %all-reduce.7.cloned.1.call-done = bf16[1024,128]{1,0:T(8,128)(2,1)} async-done(((bf16[1024,128]{1,0:T(8,128)(2,1)}), bf16[1024,128]{1,0:T(8,128)(2,1)}) %all-reduce.7.cloned.1.call-update) | async-done | bytes 262160 | tf_op jit(solution)/shard_map/while/body/eval_jaxpr/psum | solution.py:9
  1627.3 788.9 %while.39 = (s32[]{:T(128)}, f32[512,2048]{1,0:T(8,128)}, bf16[512,512]{1,0:T(8,128)(2,1)S(1)}, f32[4,128,128]{2,1,0:T(8,128)S(1)}, s32[]{:T(128)}, /*index=5*/s...) while((s32[]{:T(128)}, f32[512,2048]{1,0:T(8,128)}, ...), condition=%wide.region_13.14_spmd.clone, body=%wide.region_10.13_spmd.clone.sunk | while | flops 774111296 | bytes 15342384 | solution.py:86
  1702.6 119.9 %all-reduce.11.cloned.1.call-done = bf16[2048,128]{1,0:T(8,128)(2,1)} async-done(((bf16[2048,128]{1,0:T(8,128)(2,1)}), bf16[2048,128]{1,0:T(8,128)(2,1)}) %all-reduce.11.cloned.1.call-update) | async-done | bytes 524304 | tf_op jit(solution)/shard_map/while/body/eval_jaxpr/psum | solution.py:9
  1899.0 119.8 %all-reduce.11.cloned.1.call-done = bf16[2048,128]{1,0:T(8,128)(2,1)} async-done(((bf16[2048,128]{1,0:T(8,128)(2,1)}), bf16[2048,128]{1,0:T(8,128)(2,1)}) %all-reduce.11.cloned.1.call-update) | async-done | bytes 524304 | tf_op jit(solution)/shard_map/while/body/eval_jaxpr/psum | solution.py:9
  2095.3 119.8 %all-reduce.11.cloned.1.call-done = bf16[2048,128]{1,0:T(8,128)(2,1)} async-done(((bf16[2048,128]{1,0:T(8,128)(2,1)}), bf16[2048,128]{1,0:T(8,128)(2,1)}) %all-reduce.11.cloned.1.call-update) | async-done | bytes 524304 | tf_op jit(solution)/shard_map/while/body/eval_jaxpr/psum | solution.py:9
  2291.3 119.9 %all-reduce.11.cloned.1.call-done = bf16[2048,128]{1,0:T(8,128)(2,1)} async-done(((bf16[2048,128]{1,0:T(8,128)(2,1)}), bf16[2048,128]{1,0:T(8,128)(2,1)}) %all-reduce.11.cloned.1.call-update) | async-done | bytes 524304 | tf_op jit(solution)/shard_map/while/body/eval_jaxpr/psum | solution.py:9
  (233 shorter events, 617.3 us)
Async XLA Ops:
  10.8 79.1 %all-reduce.7.cloned.1.call-start = ((), (), s32[]{:S(2)}) async-start(), calls=%async_computation.1 | async-start | bytes 524288 | tf_op jit(solution)/shard_map/while/body/eval_jaxpr/psum | solution.py:9
  13.5 152.1 %all-reduce.5.cloned.1.call-start = ((), (), s32[]{:S(2)}) async-start(), calls=%async_computation | async-start | bytes 262144 | tf_op jit(solution)/shard_map/while/body/eval_jaxpr/psum | solution.py:9
  168.8 79.9 %all-reduce.7.cloned.1.call-start = ((), (), s32[]{:S(2)}) async-start(), calls=%async_computation.1 | async-start | bytes 524288 | tf_op jit(solution)/shard_map/while/body/eval_jaxpr/psum | solution.py:9
  171.6 152.7 %all-reduce.5.cloned.1.call-start = ((), (), s32[]{:S(2)}) async-start(), calls=%async_computation | async-start | bytes 262144 | tf_op jit(solution)/shard_map/while/body/eval_jaxpr/psum | solution.py:9
  327.5 79.5 %all-reduce.7.cloned.1.call-start = ((), (), s32[]{:S(2)}) async-start(), calls=%async_computation.1 | async-start | bytes 524288 | tf_op jit(solution)/shard_map/while/body/eval_jaxpr/psum | solution.py:9
  330.3 152.3 %all-reduce.5.cloned.1.call-start = ((), (), s32[]{:S(2)}) async-start(), calls=%async_computation | async-start | bytes 262144 | tf_op jit(solution)/shard_map/while/body/eval_jaxpr/psum | solution.py:9
  485.8 79.9 %all-reduce.7.cloned.1.call-start = ((), (), s32[]{:S(2)}) async-start(), calls=%async_computation.1 | async-start | bytes 524288 | tf_op jit(solution)/shard_map/while/body/eval_jaxpr/psum | solution.py:9
  488.6 152.8 %all-reduce.5.cloned.1.call-start = ((), (), s32[]{:S(2)}) async-start(), calls=%async_computation | async-start | bytes 262144 | tf_op jit(solution)/shard_map/while/body/eval_jaxpr/psum | solution.py:9
  644.6 79.8 %all-reduce.7.cloned.1.call-start = ((), (), s32[]{:S(2)}) async-start(), calls=%async_computation.1 | async-start | bytes 524288 | tf_op jit(solution)/shard_map/while/body/eval_jaxpr/psum | solution.py:9
  647.4 152.6 %all-reduce.5.cloned.1.call-start = ((), (), s32[]{:S(2)}) async-start(), calls=%async_computation | async-start | bytes 262144 | tf_op jit(solution)/shard_map/while/body/eval_jaxpr/psum | solution.py:9
  803.2 79.8 %all-reduce.7.cloned.1.call-start = ((), (), s32[]{:S(2)}) async-start(), calls=%async_computation.1 | async-start | bytes 524288 | tf_op jit(solution)/shard_map/while/body/eval_jaxpr/psum | solution.py:9
  806.0 152.7 %all-reduce.5.cloned.1.call-start = ((), (), s32[]{:S(2)}) async-start(), calls=%async_computation | async-start | bytes 262144 | tf_op jit(solution)/shard_map/while/body/eval_jaxpr/psum | solution.py:9
  961.8 79.9 %all-reduce.7.cloned.1.call-start = ((), (), s32[]{:S(2)}) async-start(), calls=%async_computation.1 | async-start | bytes 524288 | tf_op jit(solution)/shard_map/while/body/eval_jaxpr/psum | solution.py:9
  964.6 152.7 %all-reduce.5.cloned.1.call-start = ((), (), s32[]{:S(2)}) async-start(), calls=%async_computation | async-start | bytes 262144 | tf_op jit(solution)/shard_map/while/body/eval_jaxpr/psum | solution.py:9
  1120.5 79.5 %all-reduce.7.cloned.1.call-start = ((), (), s32[]{:S(2)}) async-start(), calls=%async_computation.1 | async-start | bytes 524288 | tf_op jit(solution)/shard_map/while/body/eval_jaxpr/psum | solution.py:9
  1123.3 152.3 %all-reduce.5.cloned.1.call-start = ((), (), s32[]{:S(2)}) async-start(), calls=%async_computation | async-start | bytes 262144 | tf_op jit(solution)/shard_map/while/body/eval_jaxpr/psum | solution.py:9
  1278.8 79.6 %all-reduce.7.cloned.1.call-start = ((), (), s32[]{:S(2)}) async-start(), calls=%async_computation.1 | async-start | bytes 524288 | tf_op jit(solution)/shard_map/while/body/eval_jaxpr/psum | solution.py:9
  1281.6 152.4 %all-reduce.5.cloned.1.call-start = ((), (), s32[]{:S(2)}) async-start(), calls=%async_computation | async-start | bytes 262144 | tf_op jit(solution)/shard_map/while/body/eval_jaxpr/psum | solution.py:9
  1437.1 79.9 %all-reduce.7.cloned.1.call-start = ((), (), s32[]{:S(2)}) async-start(), calls=%async_computation.1 | async-start | bytes 524288 | tf_op jit(solution)/shard_map/while/body/eval_jaxpr/psum | solution.py:9
  1439.9 152.7 %all-reduce.5.cloned.1.call-start = ((), (), s32[]{:S(2)}) async-start(), calls=%async_computation | async-start | bytes 262144 | tf_op jit(solution)/shard_map/while/body/eval_jaxpr/psum | solution.py:9
  1629.7 192.8 %all-reduce.11.cloned.1.call-start = ((), (), s32[]{:S(2)}) async-start(), calls=%async_computation.3 | async-start | bytes 1048576 | tf_op jit(solution)/shard_map/while/body/eval_jaxpr/psum | solution.py:9
  1829.7 189.2 %all-reduce.11.cloned.1.call-start = ((), (), s32[]{:S(2)}) async-start(), calls=%async_computation.3 | async-start | bytes 1048576 | tf_op jit(solution)/shard_map/while/body/eval_jaxpr/psum | solution.py:9
  2026.0 189.2 %all-reduce.11.cloned.1.call-start = ((), (), s32[]{:S(2)}) async-start(), calls=%async_computation.3 | async-start | bytes 1048576 | tf_op jit(solution)/shard_map/while/body/eval_jaxpr/psum | solution.py:9
  2222.2 189.0 %all-reduce.11.cloned.1.call-start = ((), (), s32[]{:S(2)}) async-start(), calls=%async_computation.3 | async-start | bytes 1048576 | tf_op jit(solution)/shard_map/while/body/eval_jaxpr/psum | solution.py:9
  (20 other events, 1089.8 us)
Sparse Core Ops, SparseCore 0:
  15.0 74.8 all-reduce.6
  97.2 68.3 all-reduce.4
  173.0 75.6 all-reduce.6
  256.0 68.2 all-reduce.4
  331.4 75.5 all-reduce.6
  414.3 68.2 all-reduce.4
  490.0 75.6 all-reduce.6
  573.0 68.3 all-reduce.4
  648.8 75.5 all-reduce.6
  807.4 75.5 all-reduce.6
  890.4 68.2 all-reduce.4
  966.1 75.5 all-reduce.6
  1049.0 68.2 all-reduce.4
  1124.4 75.5 all-reduce.6
  1207.3 68.2 all-reduce.4
  1282.7 75.6 all-reduce.6
  1365.7 68.2 all-reduce.4
  1441.4 75.5 all-reduce.6
  1524.3 68.2 all-reduce.4
  1631.3 70.3 all-reduce.8
  1705.8 116.7 all-reduce.10
  1902.0 116.7 all-reduce.10
  2098.3 116.7 all-reduce.10
  2294.4 116.7 all-reduce.10
  (4 shorter events, 268.3 us)
where the time goes:
time: 2430 us
  waiting for transfers between devices  2190 us (90%)
  matrix products  111 us (5%)
  starting transfers between devices  55 us (2%)
  local copies, waits for them, and re-layouts  34.8 us (1%)
    psum x28, waiting for transfers between devices, from_root(): return lax.psum(block, axis)  2190 us
    ppermute x11, starting transfers between devices, from_partner(): return lax.ppermute(value, axis, pairs)  54 us
  transfers between devices with their start and end apart: 39, of which 28 were waited for; matrix products, arithmetic and copies ran while one was open for 3% of the time, Pallas kernels for 0%

commit v1 on v0

v1 whole, which is shorter than its diff:
```python
import functools

import jax
import jax.numpy as jnp
from jax import lax
from jax.experimental import pallas as pl
from jax.experimental.pallas import tpu as pltpu
from jax.sharding import PartitionSpec as P

B = 128
KC = 10
KR = 4
CS = 7
RS = 16
MESH = pl.DeviceIdType.MESH
BF = jnp.bfloat16
F32 = jnp.float32


def dot_nn(left, right):
    return lax.dot_general(left, right, (((1,), (0,)), ((), ())), preferred_element_type=F32)


def dot_nt(left, right):
    return lax.dot_general(left, right, (((1,), (1,)), ((), ())), preferred_element_type=F32)


def split(value):
    high = value.astype(BF)
    return high, (value - high.astype(F32)).astype(BF)


def times_pivot(value, pivot):
    high, low = split(value)
    pivot_high, pivot_low = split(pivot)
    return dot_nn(high, pivot_high) + (dot_nn(high, pivot_low) + dot_nn(low, pivot_high))


def pivot_times(pivot_t, value):
    high, low = split(value)
    pivot_high, pivot_low = split(pivot_t)
    return dot_nn(pivot_high, high) + (dot_nn(pivot_high, low) + dot_nn(pivot_low, high))


def position():
    cube = lax.axis_index("cube")
    return cube // 2, cube % 2, lax.axis_index("row"), lax.axis_index("col")


def gather_kernel(
    colt, rowt, rcolt, rrowt, top, down, side, rtop, rdown, rside,
    local_sem, tz_send, tz_recv, tp_send, tp_recv, rp_send, rp_recv, ring_send, ring_recv,
    rtz_send, rtz_recv, rtp_send, rtp_recv, rrp_send, rrp_recv, rring_send, rring_recv, sib_send,
):
    child, half, row, col = position()
    cube = lax.axis_index("cube")
    mine = half * 8 + row
    sibling = (child * 2 + 1 - half, row, col)
    barrier = pltpu.get_barrier_semaphore()

    def greet_line(step, carry):
        pl.semaphore_signal(
            barrier, inc=1, device_id=(cube, row, (col + step) % 8), device_id_type=MESH
        )
        return carry

    def greet_plane(step, carry):
        place = (cube * 8 + row + step) % 32
        pl.semaphore_signal(
            barrier, inc=1, device_id=(place // 8, place % 8, col), device_id_type=MESH
        )
        return carry

    lax.fori_loop(1, 8, greet_line, 0)
    lax.fori_loop(1, 32, greet_plane, 0)
    pl.semaphore_wait(barrier, 38)

    def remote(source, target, send, recv, device):
        return pltpu.make_async_remote_copy(
            src_ref=source, dst_ref=target, send_sem=send, recv_sem=recv,
            device_id=device, device_id_type=MESH,
        )

    def landed(ref, recv):
        remote(ref, ref, sib_send.at[0], recv, sibling).wait_recv()

    locals_ = []

    def local(cond, source, target):
        copy = pltpu.make_async_copy(source, target, local_sem.at[len(locals_)])
        locals_.append((cond, copy))
        pl.when(cond)(copy.start)

    owns = mine < KC
    rowner = (cube == 0) & (row < KR)
    for extra in range(2):
        index = col + 8 * extra
        cond = owns & (index <= mine) & (index < KC)
        local(cond, colt.at[extra, pl.ds(0, B)], top.at[mine % KC, index % KC])

        @pl.when(cond)
        def _():
            def send(step, carry):
                remote(
                    colt.at[extra, pl.ds(0, B)], top.at[mine % KC, index % KC],
                    tz_send.at[extra * 8 + step], tz_recv.at[index % KC],
                    (cube, row, (col + step) % 8),
                ).start()
                return carry

            lax.fori_loop(1, 8, send, 0)

    rcond = rowner & (col <= row) & (col < KR)
    local(rcond, rcolt.at[pl.ds(0, B)], rtop.at[row % KR, col % KR])

    @pl.when(rcond)
    def _():
        def send(step, carry):
            remote(
                rcolt.at[pl.ds(0, B)], rtop.at[row % KR, col % KR],
                rtz_send.at[step], rtz_recv.at[col % KR], (cube, row, (col + step) % 8),
            ).start()
            return carry

        lax.fori_loop(1, 8, send, 0)

    right = (cube, row, (col + 1) % 8)
    left = (cube, row, (col + 7) % 8)
    sends = []

    def ring(cond, source, buffer, slot, send, recv, device):
        copy = remote(source, buffer.at[slot], send, recv.at[slot], device)
        sends.append((cond, copy))
        pl.when(cond)(copy.start)

    always = col >= 0
    local(always, colt.at[0], down.at[col])
    local(col < 2, colt.at[1], down.at[8 + col % 2])
    local(col < KR, rcolt, rdown.at[col % KR])
    for way, device in ((0, right), (1, left)):
        ring(always, colt.at[0], down, col, ring_send.at[way], ring_recv, device)
        ring(col < 2, colt.at[1], down, 8 + col % 2, ring_send.at[8 + way], ring_recv, device)

    for i in range(KC):
        @pl.when(owns & (mine == i))
        def _():
            for index in range(i + 1):
                @pl.when(index % 8 != col)
                def _():
                    landed(top.at[i, index], tz_recv.at[index])

            block = top.at[i, pl.ds(0, i + 1)]
            for extra in range(2):
                @pl.when((col + 8 * extra <= i))
                def _():
                    locals_[extra][1].wait()

            def send(step, carry):
                remote(
                    block, block, tp_send.at[step], tp_recv.at[i],
                    (child * 2 + i % 2, (row + step) % 8, col),
                ).start()
                return carry

            lax.fori_loop(1, 8, send, 0)
            remote(block, block, tp_send.at[0], tp_recv.at[i], sibling).start()

    local(owns, rowt, side.at[mine % KC])

    @pl.when(owns)
    def _():
        target = side.at[mine % KC]

        def send(step, carry):
            remote(
                rowt, target, rp_send.at[step], rp_recv.at[mine % KC],
                (child * 2 + mine % 2, (row + step) % 8, col),
            ).start()
            return carry

        lax.fori_loop(1, 8, send, 0)
        remote(rowt, target, rp_send.at[0], rp_recv.at[mine % KC], sibling).start()

    def ring_step(step):
        for way, device in ((0, right), (1, left)):
            slot = (col + (8 - step if way == 0 else step)) % 8
            last = 4 if way == 0 else 3
            if step > last:
                continue
            landed(down.at[slot], ring_recv.at[slot])
            if step < last:
                ring(always, down.at[slot], down, slot, ring_send.at[step * 2 + way], ring_recv, device)
            more = slot < 2
            slot2 = 8 + slot % 2

            @pl.when(more)
            def _():
                landed(down.at[slot2], ring_recv.at[slot2])

            if step < last:
                ring(more, down.at[slot2], down, slot2, ring_send.at[8 + step * 2 + way], ring_recv, device)

    def root_step(step):
        for way, device in ((0, right), (1, left)):
            slot = (col + (8 - step if way == 0 else step)) % 8
            last = 4 if way == 0 else 3
            if step > last:
                continue
            more = slot < KR
            if step > 0:
                @pl.when(more)
                def _():
                    landed(rdown.at[slot % KR], rring_recv.at[slot % KR])
            if step < last:
                source = rcolt if step == 0 else rdown.at[slot % KR]
                ring(more, source, rdown, slot % KR, rring_send.at[step * 2 + way], rring_recv, device)

    def spread(buffer, slot, block, recv, index):
        here = (row != index % 8) | (half != index // 8)
        onward = (row != index % 8) & (half == slot % 2)

        @pl.when(here)
        def _():
            landed(block, recv.at[slot])

        copy = remote(block, block, sib_send.at[buffer * KC + slot], recv.at[slot], sibling)
        sends.append((onward, copy))
        pl.when(onward)(copy.start)

    ring_step(1)
    ring_step(2)
    for i in range(KC):
        spread(0, i, top.at[i, pl.ds(0, i + 1)], tp_recv, i)
    ring_step(3)
    ring_step(4)
    for i in range(KR):
        @pl.when(rowner & (row == i))
        def _():
            for index in range(i + 1):
                @pl.when(index != col)
                def _():
                    landed(rtop.at[i, index], rtz_recv.at[index])

            @pl.when(col <= i)
            def _():
                locals_[2][1].wait()

            block = rtop.at[i, pl.ds(0, i + 1)]

            def send(step, carry):
                place = (row + step) % 16
                device = (place // 8 * 2 + i % 2, place % 8, col)
                remote(block, block, rtp_send.at[step], rtp_recv.at[i], device).start()
                remote(rrowt, rside.at[i], rrp_send.at[step], rrp_recv.at[i], device).start()
                return carry

            lax.fori_loop(1, 16, send, 0)
            remote(block, block, rtp_send.at[0], rtp_recv.at[i], sibling).start()
            remote(rrowt, rside.at[i], rrp_send.at[0], rrp_recv.at[i], sibling).start()

    local(rowner, rrowt, rside.at[row % KR])
    for i in range(KC):
        spread(1, i, side.at[i], rp_recv, i)
    for step in range(5):
        root_step(step)

    def root_spread(kind, i, block, recv):
        same_chip = (child == 0) & (row == i)
        here = jnp.logical_not(same_chip & (half == 0))
        onward = jnp.logical_not(same_chip) & (half == i % 2)

        @pl.when(here)
        def _():
            landed(block, recv.at[i])

        copy = remote(block, block, sib_send.at[(2 + kind) * KC + i], recv.at[i], sibling)
        sends.append((onward, copy))
        pl.when(onward)(copy.start)

    for i in range(KR):
        root_spread(0, i, rtop.at[i, pl.ds(0, i + 1)], rtp_recv)
    for i in range(KR):
        root_spread(1, i, rside.at[i], rrp_recv)

    for number, (cond, copy) in enumerate(locals_):
        if number > 2:
            pl.when(cond)(copy.wait)
    for cond, copy in sends:
        pl.when(cond)(copy.wait_send)
    for extra in range(2):
        index = col + 8 * extra

        @pl.when(owns & (index <= mine) & (index < KC))
        def _():
            def drain(step, carry):
                remote(
                    colt.at[extra, pl.ds(0, B)], top.at[mine % KC, index % KC],
                    tz_send.at[extra * 8 + step], tz_recv.at[index % KC], sibling,
                ).wait_send()
                return carry

            lax.fori_loop(1, 8, drain, 0)

    @pl.when(rcond)
    def _():
        def drain(step, carry):
            remote(
                rcolt.at[pl.ds(0, B)], rtop.at[row % KR, col % KR],
                rtz_send.at[step], rtz_recv.at[0], sibling,
            ).wait_send()
            return carry

        lax.fori_loop(1, 8, drain, 0)

    for i in range(KC):
        @pl.when(owns & (mine == i))
        def _():
            block = top.at[i, pl.ds(0, i + 1)]

            def drain(step, carry):
                remote(block, block, tp_send.at[step], tp_recv.at[i], sibling).wait_send()
                remote(rowt, side.at[i], rp_send.at[step], rp_recv.at[i], sibling).wait_send()
                return carry

            lax.fori_loop(0, 8, drain, 0)

    for i in range(KR):
        @pl.when(rowner & (row == i))
        def _():
            block = rtop.at[i, pl.ds(0, i + 1)]

            def drain(step, carry):
                remote(block, block, rtp_send.at[step], rtp_recv.at[i], sibling).wait_send()
                remote(rrowt, rside.at[i], rrp_send.at[step], rrp_recv.at[i], sibling).wait_send()
                return carry

            lax.fori_loop(0, 16, drain, 0)


def gather(colt, rowt, rcolt, rrowt):
    dma = pltpu.SemaphoreType.DMA
    shapes = [
        (KC, KC, B, B), (KC, 4 * B, B), (KC, B, CS * B),
        (KR, KR, B, B), (KR, 4 * B, B), (KR, B, RS * B),
    ]
    return pl.pallas_call(
        gather_kernel,
        out_shape=[jax.ShapeDtypeStruct(shape, BF) for shape in shapes],
        in_specs=[pl.BlockSpec(memory_space=pl.ANY)] * 4,
        out_specs=[pl.BlockSpec(memory_space=pl.ANY)] * 6,
        scratch_shapes=[
            dma((8,)), dma((16,)), dma((KC,)), dma((8,)), dma((KC,)), dma((8,)), dma((KC,)),
            dma((16,)), dma((KC,)),
            dma((8,)), dma((KR,)), dma((16,)), dma((KR,)), dma((16,)), dma((KR,)), dma((8,)), dma((KR,)),
            dma((4 * KC,)),
        ],
        compiler_params=pltpu.CompilerParams(collective_id=0, has_side_effects=True),
    )(colt, rowt, rcolt, rrowt)


def factor(count, top, down, side, pivots, panels_top, panels, wide, row_class, first_tile):
    rows = panels.shape[0]
    columns = wide.shape[1]
    row_block = lax.broadcasted_iota(jnp.int32, (rows, B), 0) < B
    col_block = lax.broadcasted_iota(jnp.int32, (B, columns), 1) < B
    for pair in range(count // 2):
        k = 2 * pair
        at = k * B
        here, there = slice(at, at + B), slice(at + B, at + 2 * B)
        pivot, pivot2 = pivots[k], pivots[k + 1]
        pivot_t, pivot2_t = pivot.T, pivot2.T
        length = (count - k) * B
        first = top[k:count, k].reshape(length, B).astype(F32)
        second = top[k + 1:count, k + 1].reshape(length - B, B).astype(F32)
        own = down[k].astype(F32)
        own2 = down[k + 1].astype(F32)
        across = side[k].astype(F32)
        across2 = side[k + 1].astype(F32)
        if pair:
            lead = panels_top[at:at + 2 * B, :at]
            both = dot_nt(panels_top[at:, :at], lead)
            first = first - both[:, :B]
            second = second - both[B:, B:]
            both = dot_nt(panels[:, :at], lead)
            own = own - both[:, :B]
            own2 = own2 - both[:, B:]
            both = dot_nn(lead, wide[:at, :])
            across = across - both[:B]
            across2 = across2 - both[B:]
        first = times_pivot(first, pivot).astype(BF)
        panels_top[at:, here] = first
        link = first[B:2 * B]
        second = times_pivot(second - dot_nt(first[B:], link), pivot2).astype(BF)
        panels_top[at + B:, there] = second
        own = times_pivot(own, pivot)
        own = jnp.where(row_block & (row_class < k), 0.0, own).astype(BF)
        panels[:, here] = own
        own2 = times_pivot(own2 - dot_nt(own, link), pivot2)
        own2 = jnp.where(row_block & (row_class < k + 1), 0.0, own2).astype(BF)
        panels[:, there] = own2
        across = pivot_times(pivot_t, across)
        across = jnp.where(col_block & (first_tile < k), 0.0, across).astype(BF)
        wide[here, :] = across
        across2 = pivot_times(pivot2_t, across2 - dot_nn(link, across))
        across2 = jnp.where(col_block & (first_tile < k + 1), 0.0, across2).astype(BF)
        wide[there, :] = across2


def child_kernel(top, down, side, pivots, front, panels_out, keep, away, panels_top, wide, update):
    child, half, row, col = position()
    factor(KC, top, down, side, pivots, panels_top, panels_out, wide, half * 8 + row, 8 + col)
    for t in range(4):
        block = slice(t * B, (t + 1) * B)
        value = front[block, :].astype(F32) - dot_nn(panels_out[block, :], wide[...])
        update[t] = value.astype(BF)
    for p in range(2):
        keep[p] = update[2 * p + child]
        away[p] = update[2 * p + 1 - child]


def child_step(top, down, side, pivots, front):
    vmem = pl.BlockSpec(memory_space=pltpu.VMEM)
    return pl.pallas_call(
        child_kernel,
        out_shape=[
            jax.ShapeDtypeStruct((4 * B, KC * B), BF),
            jax.ShapeDtypeStruct((2, B, CS * B), BF),
            jax.ShapeDtypeStruct((2, B, CS * B), BF),
        ],
        in_specs=[vmem] * 5,
        out_specs=[vmem] * 3,
        scratch_shapes=[
            pltpu.VMEM((KC * B, KC * B), BF),
            pltpu.VMEM((KC * B, CS * B), BF),
            pltpu.VMEM((4, B, CS * B), BF),
        ],
        compiler_params=pltpu.CompilerParams(vmem_limit_bytes=48 * 2**20),
        cost_estimate=pl.CostEstimate(flops=8 * 10**9, bytes_accessed=10**7, transcendentals=0),
    )(top, down, side, pivots, front)


def root_kernel(top, down, side, pivots, front, panels_out, rest, panels_top, wide):
    child, half, row, col = position()
    factor(KR, top, down, side, pivots, panels_top, panels_out, wide, (child * 2 + half) * 8 + row, col)
    for t in range(4):
        block = slice(t * B, (t + 1) * B)
        rest[block, :] = front[block, :].astype(F32) - dot_nn(panels_out[block, :], wide[...])


def root_step(top, down, side, pivots, front):
    vmem = pl.BlockSpec(memory_space=pltpu.VMEM)
    return pl.pallas_call(
        root_kernel,
        out_shape=[
            jax.ShapeDtypeStruct((4 * B, KR * B), BF),
            jax.ShapeDtypeStruct((4 * B, RS * B), F32),
        ],
        in_specs=[vmem] * 5,
        out_specs=[vmem] * 2,
        scratch_shapes=[pltpu.VMEM((KR * B, KR * B), BF), pltpu.VMEM((KR * B, RS * B), BF)],
        compiler_params=pltpu.CompilerParams(vmem_limit_bytes=48 * 2**20),
        cost_estimate=pl.CostEstimate(flops=3 * 10**9, bytes_accessed=10**7, transcendentals=0),
    )(top, down, side, pivots, front)


def add_kernel(maps, rest, keep, came, out, total):
    child, half, row, col = position()
    total[...] = rest[...]
    for source, tiles in ((child, keep), (1 - child, came)):
        for p in range(2):
            i = (2 * p + child) * 16 + half * 8 + row - KC
            for s in range(1, 8):
                j = s * 8 + col - KC

                @pl.when((i >= 0) & (j >= 0))
                def _():
                    down = maps[source, jnp.maximum(i, 0)] // 32
                    across = maps[source, jnp.maximum(j, 0)] // 8
                    at = (pl.ds(pl.multiple_of(down * B, B), B), pl.ds(pl.multiple_of(across * B, B), B))
                    total[at] += tiles[p, :, (s - 1) * B:s * B].astype(F32)
    for t in range(4):
        for b in range(0, B, 32):
            value = total[t * B + b:t * B + b + 32, :].reshape(32, RS, B)
            out[t, b:b + 32] = value.astype(BF)


def add_step(maps, rest, keep, came):
    vmem = pl.BlockSpec(memory_space=pltpu.VMEM)
    return pl.pallas_call(
        add_kernel,
        out_shape=jax.ShapeDtypeStruct((4, B, RS, B), BF),
        in_specs=[pl.BlockSpec(memory_space=pltpu.SMEM)] + [vmem] * 3,
        out_specs=vmem,
        scratch_shapes=[pltpu.VMEM((4 * B, RS * B), F32)],
        compiler_params=pltpu.CompilerParams(vmem_limit_bytes=48 * 2**20),
    )(maps, rest, keep, came)


def on_device(child_fronts, root_front, child_pivots, root_pivots, child_maps):
    child = lax.axis_index("cube") // 2
    fronts = child_fronts.reshape(4, B, 8, B)
    roots = root_front.reshape(4, B, RS, B)
    colt = fronts[:, :, :2, :].transpose(2, 0, 1, 3).reshape(2, 4 * B, B)
    rowt = fronts[0, :, 1:, :].reshape(B, CS * B)
    rcolt = roots[:, :, 0, :].reshape(4 * B, B)
    rrowt = roots[0].reshape(B, RS * B)
    front = fronts[:, :, 1:, :].reshape(4 * B, CS * B)
    root = roots.reshape(4 * B, RS * B)
    top, down, side, rtop, rdown, rside = gather(colt, rowt, rcolt, rrowt)
    pivots = lax.dynamic_index_in_dim(child_pivots, child, 0, keepdims=False)
    panels, keep, away = child_step(top, down, side, pivots, front)
    pairs = [(source, source ^ 2) for source in range(4)]
    came = lax.ppermute(away, "cube", pairs)
    root_panels, rest = root_step(rtop, rdown, rside, root_pivots, root)
    root_rest = add_step(child_maps, rest, keep, came)
    return (
        panels.reshape(4, 1, B, KC * B),
        root_panels.reshape(4, 1, B, KR * B),
        root_rest.reshape(4, 1, B, RS, 1, B),
    )


def solution(mesh):
    placed = (
        P(None, ("cube", "row"), None, None, "col", None),
        P(None, ("cube", "row"), None, None, "col", None),
        P(),
        P(),
        P(),
    )
    return jax.shard_map(
        on_device,
        mesh=mesh,
        in_specs=placed,
        out_specs=(
            P(None, ("cube", "row"), None, None),
            P(None, ("cube", "row"), None, None),
            P(None, ("cube", "row"), None, None, "col", None),
        ),
        check_vma=False,
    )
```

time: 2430 us -> 178 us (0.07)
  waiting for transfers between devices: 2190 us -> 1.24 us
  Pallas kernels: 0 us -> 116 us
  matrix products: 111 us -> 0 us
    psum x28 -> x0, waiting for transfers between devices: 2190 us -> none  [from_root(): return lax.psum(block, axis)]
    pallas_call x0 -> x4, Pallas kernels: none -> 116 us  [the longest x1 91.6 us: gather(): pl.pallas_call(gather_kernel, out_shape=[jax.ShapeDtypeStruct(shape, BF)...]
    dot_general x46 -> x0, matrix products: 111 us -> none  [the longest x14 41.8 us: prepare(): lax.dot_general(across, pivot, (((0,), (0,)), ((), ())), precision=lax.Pr...]
    ppermute x11 -> x1, starting transfers between devices: 54 us -> 36 us  [on_device(): came = lax.ppermute(away, 'cube', pairs)]
  transfers between devices with their start and end apart: 39 -> 1, of which waited for: 28 -> 1; matrix products, arithmetic and copies ran while one was open for 3% -> 0% of each run, Pallas kernels for 0% -> 4%
where the time goes in v1:
time: 178 us; the launch traced here: 175 us
  Pallas kernels  116 us (65%)
  starting transfers between devices  36 us (20%)
  local copies, waits for them, and re-layouts  20.9 us (12%)
    pallas_call x1, Pallas kernels, gather(): pl.pallas_call(gather_kernel, out_shape=[jax.ShapeDtypeStruct(shape, BF)...  91.6 us
    ppermute x1, starting transfers between devices, on_device(): came = lax.ppermute(away, 'cube', pairs)  36 us
    pallas_call x1, Pallas kernels, child_step(): pl.pallas_call(child_kernel, out_shape=[jax.ShapeDtypeStruct((4 * B, KC *...  14 us
    unnamed x31, local copies, waits for them, and re-layouts  12.6 us
    pallas_call x1, Pallas kernels, root_step(): pl.pallas_call(root_kernel, out_shape=[jax.ShapeDtypeStruct((4 * B, KR *...  7.14 us
  transfers between devices with their start and end apart: 1, of which 1 were waited for; matrix products, arithmetic and copies ran while one was open for 0% of the time, Pallas kernels for 4%

profile of v1, /device:TPU:25, one launch (start us, length us, event | category | flops | bytes accessed | tf_op | source)
XLA Modules:
  0.0 175.3 jit_solution(11385895725504868196)
XLA Ops:
  0.7 2.6 %copy.12 = bf16[4,1,128,8,1,128]{2,5,3,0,4,1:T(8,128)(2,1)} copy(bf16[4,1,128,8,1,128]{5,3,4,2,1,0:T(8,128)(2,1)} %param.5) | data formatting | bytes 2097152 | tf_op args[0]
  3.2 1.7 slice_bitcast_fusion
  4.9 1.6 slice.22
  6.5 1.9 %copy.31 = bf16[4,1,128,16,1,128]{5,2,0,3,4,1:T(8,128)(2,1)} copy(bf16[4,1,128,16,1,128]{5,3,4,2,1,0:T(8,128)(2,1)S(1)} %copy-done.9) | data formatting | bytes 4194304 | tf_op args[1]
  8.5 1.9 %copy.13 = bf16[2,4,128,128]{3,2,1,0:T(8,128)(2,1)} copy(bf16[2,4,128,128]{2,3,0,1:T(8,128)(2,1)} %slice_bitcast_fusion) | data formatting | bytes 524288 | tf_op jit(solution)/shard_map/transpose | solution.py:503
  10.4 0.8 copy.15.rowt
  11.2 1.6 slice.23
  12.8 0.9 copy.33
  13.7 0.7 copy.21
  14.4 0.1 copy.32
  14.6 91.6 %shard_map.76 = (bf16[10,10,128,128]{3,2,1,0:T(8,128)(2,1)}, bf16[10,512,128]{2,1,0:T(8,128)(2,1)}, bf16[10,128,896]{2,1,0:T(8,128)(2,1)}, bf16[4,4,128,128]{3,2...) custom-call(bf16[2,512,128]{2,1,0:T(8,128)(2,1)} %bitcast.48, ...), custom_call_target="tpu_custom_call" | custom-call | tf_op jit(solution)/shard_map/pallas_call | solution.py:346
  106.2 1.6 copy-done.3
  107.9 1.3 copy-done.5
  109.2 14.0 %shard_map.77 = (bf16[512,1280]{1,0:T(8,128)(2,1)}, bf16[2,128,896]{2,1,0:T(8,128)(2,1)S(1)}, bf16[2,128,896]{2,1,0:T(8,128)(2,1)S(1)}) custom-call(bf16[10,10,128,128]{3,2,1,0:T(8,128)(2,1)} %get-tuple-element.14.top, bf16[10,512,128]{2,1,0:T(8,128)(2,1)S(1)} %copy-done.5, bf16[10,128,896]{2,1,0:T(8,128)(2,1)S(1)} %copy-done.3, ...), custom_call_target="tpu_custom_call" | custom-call | flops 8000000000 | bytes 10000000 | tf_op jit(solution)/shard_map/pallas_call | solution.py:423
  123.2 36.0 %collective-permute-start = (bf16[2,128,896]{2,1,0:T(8,128)(2,1)S(1)}, bf16[2,128,896]{2,1,0:T(8,128)(2,1)S(1)}, u32[]{:S(2)}, u32[]{:S(2)}) collective-permute-start(bf16[2,128,896]{2,1,0:T(8,128)(2,1)S(1)} %get-tuple-element.24), channel_id=1, source_target_pairs={{0,128},{64,192},{128,0},{192,64},{1,129},{65,193},{129,1},{193,65... | collective-permute-start | bytes 1376264 | tf_op jit(solution)/shard_map/ppermute | solution.py:513
  159.3 0.5 copy.30
  159.8 1.0 copy-done.4
  160.8 0.1 copy-done.6
  160.9 0.2 copy-done.7
  161.1 0.1 copy-done.8
  161.2 7.1 %shard_map.78 = (bf16[512,512]{1,0:T(8,128)(2,1)}, f32[512,2048]{1,0:T(8,128)}) custom-call(bf16[4,4,128,128]{3,2,1,0:T(8,128)(2,1)S(1)} %copy-done.6, bf16[4,512,128]{2,1,0:T(8,128)(2,1)S(1)} %copy-done.7, bf16[4,128,2048]{2,1,0:T(8,128)(2,1)S(1)} %copy-done.4, f32[4,128,128]{2,1,0:T(8,128)S(1)} %copy-done.8, bf16[512,2048]{1,0:T(8,128)(2,1)S(1)} %bitcast.37), custom_call_target="tpu_custom_call" | custom-call | flops 3000000000 | bytes 10000000 | tf_op jit(solution)/shard_map/pallas_call | solution.py:452
  168.3 1.2 collective-permute-done.came
  169.5 2.2 %copy-done.1 = f32[512,2048]{1,0:T(8,128)S(1)} copy-done((f32[512,2048]{1,0:T(8,128)S(1)}, f32[512,2048]{1,0:T(8,128)}, u32[]{:S(2)}) %copy-start.1) | copy-done | bytes 4194328
  171.7 3.5 %shard_map.79 = bf16[4,128,16,128]{3,2,1,0:T(8,128)(2,1)} custom-call(s32[2,54]{1,0:T(2,128)S(1)} %copy-done.2, f32[512,2048]{1,0:T(8,128)S(1)} %copy-done.1, bf16[2,128,896]{2,1,0:T(8,128)(2,1)S(1)} %get-tuple-element.23.keep, bf16[2,128,896]{2,1,0:T(8,128)(2,1)S(1)} %collective-permute-done.came), custom_call_target="tpu_custom_call" | custom-call | tf_op jit(solution)/shard_map/pallas_call | solution.py:489
  (23 shorter events, 0.2 us)
Async XLA Ops:
  0.6 13.9 %copy-start = (f32[2,10,128,128]{3,2,1,0:T(8,128)S(1)}, f32[2,10,128,128]{3,2,1,0:T(8,128)}, u32[]{:S(2)}) copy-start(f32[2,10,128,128]{3,2,1,0:T(8,128)} %param.7) | copy-start | bytes 3932164
  0.6 5.9 %copy-start.9 = (bf16[4,1,128,16,1,128]{5,3,4,2,1,0:T(8,128)(2,1)S(1)}, bf16[4,1,128,16,1,128]{5,3,4,2,1,0:T(8,128)(2,1)}, u32[]{:S(2)}) copy-start(bf16[4,1,128,16,1,128]{5,3,4,2,1,0:T(8,128)(2,1)} %param.6) | copy-start | bytes 6291460
  6.5 1.9 %copy-start.11 = (bf16[4,1,128,8,1,128]{2,5,3,0,4,1:T(8,128)(2,1)S(1)}, bf16[4,1,128,8,1,128]{2,5,3,0,4,1:T(8,128)(2,1)}, u32[]{:S(2)}) copy-start(bf16[4,1,128,8,1,128]{2,5,3,0,4,1:T(8,128)(2,1)} %copy.12) | copy-start | bytes 3145732
  8.4 1.9 %copy-start.12 = (bf16[1,128,7,128]{1,3,2,0:T(8,128)(2,1)S(1)}, bf16[1,128,7,128]{1,3,2,0:T(8,128)(2,1)}, u32[]{:S(2)}) copy-start(bf16[1,128,7,128]{1,3,2,0:T(8,128)(2,1)} %slice.22) | copy-start | bytes 688132
  8.4 4.3 %slice-start = ((bf16[4,1,128,16,1,128]{5,3,4,2,1,0:T(8,128)(2,1)}), bf16[1,1,128,16,1,128]{5,3,4,2,1,0:T(8,128)(2,1)S(1)}, s32[]{:S(2)}) async-start(bf16[4,1,128,16,1,128]{5,3,4,2,1,0:T(8,128)(2,1)} %param.6), calls=%async_computation | async-start | bytes 1048576 | tf_op jit(solution)/shard_map/slice | solution.py:506
  106.2 1.6 copy-start.3
  107.9 1.3 copy-start.5
  109.2 50.1 %copy-start.10 = (bf16[4,1,128,16,1,128]{5,3,4,2,1,0:T(8,128)(2,1)S(1)}, bf16[4,1,128,16,1,128]{5,3,4,2,1,0:T(8,128)(2,1)}, u32[]{:S(2)}) copy-start(bf16[4,1,128,16,1,128]{5,3,4,2,1,0:T(8,128)(2,1)} %param.6) | copy-start | bytes 6291460
  123.2 46.3 %collective-permute-start = (bf16[2,128,896]{2,1,0:T(8,128)(2,1)S(1)}, bf16[2,128,896]{2,1,0:T(8,128)(2,1)S(1)}, u32[]{:S(2)}, u32[]{:S(2)}) collective-permute-start(bf16[2,128,896]{2,1,0:T(8,128)(2,1)S(1)} %get-tuple-element.24), channel_id=1, source_target_pairs={{0,128},{64,192},{128,0},{192,64},{1,129},{65,193},{129,1},{193,65... | collective-permute-start | bytes 1376264 | tf_op jit(solution)/shard_map/ppermute | solution.py:513
  159.3 1.6 copy-start.4
  159.3 1.7 copy-start.6
  159.3 1.8 %copy-start.7 = (bf16[4,512,128]{2,1,0:T(8,128)(2,1)S(1)}, bf16[4,512,128]{2,1,0:T(8,128)(2,1)}, u32[]{:S(2)}) copy-start(bf16[4,512,128]{2,1,0:T(8,128)(2,1)} %get-tuple-element.19.down) | copy-start | bytes 1572868
  159.3 1.9 %copy-start.8 = (f32[4,128,128]{2,1,0:T(8,128)S(1)}, f32[4,128,128]{2,1,0:T(8,128)}, u32[]{:S(2)}) copy-start(f32[4,128,128]{2,1,0:T(8,128)} %pivots.1) | copy-start | bytes 786436
  161.1 8.4 %copy-start.2 = (s32[2,54]{1,0:T(2,128)S(1)}, s32[2,54]{1,0:T(2,128)}, u32[]{:S(2)}) copy-start(s32[2,54]{1,0:T(2,128)} %maps.1) | copy-start | bytes 1300
  169.5 2.2 %copy-start.1 = (f32[512,2048]{1,0:T(8,128)S(1)}, f32[512,2048]{1,0:T(8,128)}, u32[]{:S(2)}) copy-start(f32[512,2048]{1,0:T(8,128)} %get-tuple-element.22.rest) | copy-start | bytes 12582916

commit v2 on v0

v2 whole, which is shorter than its diff:
```python
import functools

import jax
import jax.numpy as jnp
from jax import lax
from jax.experimental import pallas as pl
from jax.experimental.pallas import tpu as pltpu
from jax.sharding import PartitionSpec as P

B = 128
KC = 10
KR = 4
CS = 7
RS = 16
MESH = pl.DeviceIdType.MESH
BF = jnp.bfloat16
F32 = jnp.float32


def dot_nn(left, right):
    return lax.dot_general(left, right, (((1,), (0,)), ((), ())), preferred_element_type=F32)


def dot_nt(left, right):
    return lax.dot_general(left, right, (((1,), (1,)), ((), ())), preferred_element_type=F32)


def split(value):
    high = value.astype(BF)
    return high, (value - high.astype(F32)).astype(BF)


def times_pivot(value, pivot):
    high, low = split(value)
    pivot_high, pivot_low = split(pivot)
    return dot_nn(high, pivot_high) + (dot_nn(high, pivot_low) + dot_nn(low, pivot_high))


def pivot_times(pivot_t, value):
    high, low = split(value)
    pivot_high, pivot_low = split(pivot_t)
    return dot_nn(pivot_high, high) + (dot_nn(pivot_high, low) + dot_nn(pivot_low, high))


def position():
    cube = lax.axis_index("cube")
    return cube // 2, cube % 2, lax.axis_index("row"), lax.axis_index("col")


def neighbours(which):
    child, half, row, col = position()
    x, y = row // 2, child * 2 + row % 2
    if which == "x":
        return [(child * 2 + half, (x + d) % 4 * 2 + row % 2, col) for d in (1, 3, 2)]
    if which == "pair":
        return [(child * 2 + half, row + 1 - 2 * (row % 2), col)]
    places = [(y + d) % 4 for d in (1, 3, 2)]
    return [(place // 2 * 2 + half, x * 2 + place % 2, col) for place in places]


class Traffic:
    def __init__(self):
        self.pending = []

    def send(self, cond, source, target, send_sem, recv_sem, device):
        copy = pltpu.make_async_remote_copy(
            src_ref=source, dst_ref=target, send_sem=send_sem, recv_sem=recv_sem,
            device_id=device, device_id_type=MESH,
        )
        pl.when(cond)(copy.start)
        self.pending.append((cond, copy))

    def landed(self, cond, block, recv_sem):
        child, half, row, col = position()
        copy = pltpu.make_async_remote_copy(
            src_ref=block, dst_ref=block, send_sem=recv_sem, recv_sem=recv_sem,
            device_id=(child * 2 + 1 - half, row, col), device_id_type=MESH,
        )
        pl.when(cond)(copy.wait_recv)

    def drain(self):
        for cond, copy in self.pending:
            pl.when(cond)(copy.wait_send)
        self.pending = []


class Spread:
    def __init__(self, traffic, blocks, recv, send, whole):
        self.traffic, self.blocks, self.recv, self.sems = traffic, blocks, recv, send
        child, half, row, col = position()
        self.half = half
        self.sibling = (child * 2 + 1 - half, row, col)
        x, yl = row // 2, row % 2
        self.along_x = neighbours("x")
        self.along_y = neighbours("y" if whole else "pair")
        self.roles = []
        for i in range(len(blocks)):
            same_x = x == i % 8 // 2
            same_y = yl == i % 2
            if whole:
                same_y = same_y & (child == 0)
            self.roles.append((same_x, same_y, half == i // 8))

    def _out(self, cond, i, part, devices, first):
        for n, device in enumerate(devices):
            block = self.blocks[i][part]
            self.traffic.send(cond, block, block, self.sems.at[i, first + n], self.recv.at[part, i], device)

    def _wait(self, cond, i, part):
        self.traffic.landed(cond, self.blocks[i][part], self.recv.at[part, i])

    def parts(self, i):
        return [part for part in range(2) if self.blocks[i][part] is not None]

    def begin(self, i, ready):
        same_x, same_y, core = self.roles[i]
        chip = same_x & same_y
        for part in self.parts(i):
            self._out(ready & chip & core, i, part, [self.sibling], 6 + part)
        for part in self.parts(i):
            taker = self.half == part
            self._wait(chip & jnp.logical_not(core) & taker, i, part)
            one, two = (self.along_x, self.along_y) if part == 0 else (self.along_y, self.along_x)
            self._out(chip & taker, i, part, one, 0)
            self._out(chip & taker, i, part, two, 3)

    def relay(self, i):
        same_x, same_y, core = self.roles[i]
        for part in self.parts(i):
            near = (same_y & jnp.logical_not(same_x)) if part == 0 else (same_x & jnp.logical_not(same_y))
            near = near & (self.half == part)
            self._wait(near, i, part)
            self._out(near, i, part, self.along_y if part == 0 else self.along_x, 0)
            self._out(near, i, part, [self.sibling], 6)

    def settle(self, i):
        same_x, same_y, core = self.roles[i]
        for part in self.parts(i):
            far = jnp.logical_not(same_y if part == 0 else same_x) & (self.half == part)
            self._wait(far, i, part)
            self._out(far, i, part, [self.sibling], 7)

    def finish(self, i):
        same_x, same_y, core = self.roles[i]
        owner = same_x & same_y & core
        for part in self.parts(i):
            self._wait(jnp.logical_not(owner) & (self.half != part), i, part)


class Line:
    def __init__(self, traffic, buffer, count, recv, send):
        self.traffic, self.buffer, self.count, self.recv, self.sems = traffic, buffer, count, recv, send
        child, half, row, col = position()
        self.col = col
        self.place = lambda d: (child * 2 + half, row, (col + d) % 8)

    def _slots(self, step):
        base = (self.col + step) % 8
        for extra in range((self.count + 7) // 8):
            limit = min(self.count - 8 * extra, 8)
            cond = base < limit
            yield extra, cond, 8 * extra + base % limit

    def begin(self):
        for extra, cond, slot in self._slots(0):
            for n, d in enumerate((1, 7, 2, 6)):
                block = self.buffer.at[slot]
                self.traffic.send(cond, block, block, self.sems.at[extra, n], self.recv.at[slot], self.place(d))

    def relay(self):
        for n, (step, goals) in enumerate(((6, (1, 2)), (2, (7,)))):
            for extra, cond, slot in self._slots(step):
                block = self.buffer.at[slot]
                self.traffic.landed(cond, block, self.recv.at[slot])
                for m, d in enumerate(goals):
                    self.traffic.send(
                        cond, block, block, self.sems.at[extra, 4 + 2 * n + m], self.recv.at[slot], self.place(d)
                    )

    def finish(self):
        for step in (7, 1, 5, 3, 4):
            for extra, cond, slot in self._slots(step):
                self.traffic.landed(cond, self.buffer.at[slot], self.recv.at[slot])


class TopLine:
    def __init__(self, traffic, count, buffer, recv, send, owns, mine):
        child, half, row, col = position()
        self.traffic, self.count, self.buffer, self.recv, self.sems = traffic, count, buffer, recv, send
        self.owns, self.mine, self.col = owns, mine % count, col
        self.place = lambda d: (child * 2 + half, row, (col + d) % 8)

    def begin(self):
        for extra in range((self.count + 7) // 8):
            limit = min(self.count - 8 * extra, 8)
            index = 8 * extra + self.col % limit
            cond = self.owns & (self.col < limit) & (index <= self.mine)
            block = self.buffer.at[self.mine, index]
            for n, d in enumerate((1, 7, 2, 6, 3, 5, 4)):
                self.traffic.send(cond, block, block, self.sems.at[extra, n], self.recv.at[index], self.place(d))

    def finish(self):
        for index in range(self.count):
            cond = self.owns & (index <= self.mine) & (self.col != index % 8)
            self.traffic.landed(cond, self.buffer.at[self.mine, index], self.recv.at[index])


def greet_all():
    child, half, row, col = position()
    cube = child * 2 + half
    barrier = pltpu.get_barrier_semaphore()

    def greet_line(step, carry):
        pl.semaphore_signal(
            barrier, inc=1, device_id=(cube, row, (col + step) % 8), device_id_type=MESH
        )
        return carry

    lax.fori_loop(1, 8, greet_line, 0)
    others = neighbours("x") + neighbours("y") + [(child * 2 + 1 - half, row, col)]
    for device in others:
        pl.semaphore_signal(barrier, inc=1, device_id=device, device_id_type=MESH)
    return barrier, 7 + len(others)


def halves_of_tiles(buffer, count):
    blocks = []
    for i in range(count):
        middle = (i + 2) // 2
        second = buffer.at[i, pl.ds(middle, i + 1 - middle)] if i + 1 > middle else None
        blocks.append((buffer.at[i, pl.ds(0, middle)], second))
    return blocks


def halves_of_rows(buffer, count):
    return [
        (buffer.at[i, pl.ds(0, B // 2)], buffer.at[i, pl.ds(B // 2, B // 2)]) for i in range(count)
    ]


def factor_top(count, pair, top, pivots, panels):
    k = 2 * pair
    at = k * B
    length = (count - k) * B
    first = top[k:count, k].reshape(length, B).astype(F32)
    second = top[k + 1:count, k + 1].reshape(length - B, B).astype(F32)
    if pair:
        both = dot_nt(panels[at:, :at], panels[at:at + 2 * B, :at])
        first = first - both[:, :B]
        second = second - both[B:, B:]
    first = times_pivot(first, pivots[k]).astype(BF)
    panels[at:, at:at + B] = first
    second = second - dot_nt(first[B:], first[B:2 * B])
    panels[at + B:, at + B:at + 2 * B] = times_pivot(second, pivots[k + 1]).astype(BF)


def factor_own(pair, down, pivots, panels_top, panels, row_class):
    k = 2 * pair
    at = k * B
    row_block = lax.broadcasted_iota(jnp.int32, (panels.shape[0], B), 0) < B
    first = down[k].astype(F32)
    second = down[k + 1].astype(F32)
    if pair:
        both = dot_nt(panels[:, :at], panels_top[at:at + 2 * B, :at])
        first = first - both[:, :B]
        second = second - both[:, B:]
    first = times_pivot(first, pivots[k])
    first = jnp.where(row_block & (row_class < k), 0.0, first).astype(BF)
    panels[:, at:at + B] = first
    second = second - dot_nt(first, panels_top[at + B:at + 2 * B, at:at + B])
    second = times_pivot(second, pivots[k + 1])
    second = jnp.where(row_block & (row_class < k + 1), 0.0, second).astype(BF)
    panels[:, at + B:at + 2 * B] = second


def factor_wide(pair, side, pivots, panels_top, wide, first_tile):
    k = 2 * pair
    at = k * B
    col_block = lax.broadcasted_iota(jnp.int32, (B, wide.shape[1]), 1) < B
    first = side[k].astype(F32)
    second = side[k + 1].astype(F32)
    if pair:
        both = dot_nn(panels_top[at:at + 2 * B, :at], wide[:at, :])
        first = first - both[:B]
        second = second - both[B:]
    first = pivot_times(pivots[k].T, first)
    first = jnp.where(col_block & (first_tile < k), 0.0, first).astype(BF)
    wide[at:at + B, :] = first
    second = second - dot_nn(panels_top[at + B:at + 2 * B, at:at + B], first)
    second = pivot_times(pivots[k + 1].T, second)
    second = jnp.where(col_block & (first_tile < k + 1), 0.0, second).astype(BF)
    wide[at + B:at + 2 * B, :] = second


def main_kernel(
    fronts, roots, child_pivots, root_pivots,
    panels_out, root_panels_out, rest_out, keep_out, came_out,
    craw, rraw, cwide, rwide, cpiv, rpiv,
    top, down, side, rtop, rdown, rside,
    ctop, cown, cside, xtop, xown, xside, update,
    load_sem, store_sem, tl_send, tl_recv, rtl_send, rtl_recv, line_send, line_recv, rline_send, rline_recv,
    t_send, t_recv, s_send, s_recv, rt_send, rt_recv, rs_send, rs_recv, u_send, u_recv,
):
    child, half, row, col = position()
    mine = half * 8 + row
    root_class = child * 16 + mine
    owns = mine < KC
    root_owns = (child == 0) & (half == 0) & (row < KR)

    loads = [
        pltpu.make_async_copy(fronts, craw, load_sem.at[0]),
        pltpu.make_async_copy(child_pivots.at[child], cpiv, load_sem.at[1]),
        pltpu.make_async_copy(roots, rraw, load_sem.at[2]),
        pltpu.make_async_copy(root_pivots, rpiv, load_sem.at[3]),
    ]
    for load in loads:
        load.start()
    barrier, count = greet_all()

    loads[0].wait()
    for t in range(4):
        cwide[t * 8 * B:(t + 1) * 8 * B, :] = craw[t].astype(F32).reshape(8 * B, B)
    column = cwide[pl.ds(0, 4 * B, stride=8), :].astype(BF)
    down[col] = column

    @pl.when(owns & (col <= mine))
    def _():
        top[mine % KC, col] = column[:B]

    @pl.when(col < 2)
    def _():
        column2 = cwide[pl.ds(1, 4 * B, stride=8), :].astype(BF)
        down[8 + col % 2] = column2

        @pl.when(owns & (8 + col <= mine))
        def _():
            top[mine % KC, 8 + col % 2] = column2[:B]

    @pl.when(owns)
    def _():
        for s in range(CS):
            side[mine % KC, :, s * B:(s + 1) * B] = cwide[pl.ds(s + 1, B, stride=8), :].astype(BF)

    loads[2].wait()
    for t in range(4):
        for b in range(0, B, 32):
            at = (t * B + b) * RS
            rwide[at:at + 32 * RS, :] = rraw[t, b:b + 32].astype(F32).reshape(32 * RS, B)

    @pl.when(col < KR)
    def _():
        root_column = rwide[pl.ds(0, 4 * B, stride=RS), :].astype(BF)
        rdown[col % KR] = root_column

        @pl.when(root_owns & (col <= row))
        def _():
            rtop[row % KR, col % KR] = root_column[:B]

    @pl.when(root_owns)
    def _():
        for s in range(RS):
            rside[row % KR, :, s * B:(s + 1) * B] = rwide[pl.ds(s, B, stride=RS), :].astype(BF)

    traffic = Traffic()
    top_line = TopLine(traffic, KC, top, tl_recv, tl_send, owns, mine)
    root_top_line = TopLine(traffic, KR, rtop, rtl_recv, rtl_send, root_owns, row)
    line = Line(traffic, down, KC, line_recv, line_send)
    root_line = Line(traffic, rdown, KR, rline_recv, rline_send)
    top_spread = Spread(traffic, halves_of_tiles(top, KC), t_recv, t_send, False)
    side_spread = Spread(traffic, halves_of_rows(side, KC), s_recv, s_send, False)
    root_top_spread = Spread(traffic, halves_of_tiles(rtop, KR), rt_recv, rt_send, True)
    root_side_spread = Spread(traffic, halves_of_rows(rside, KR), rs_recv, rs_send, True)
    always = col >= 0

    pl.semaphore_wait(barrier, count)
    top_line.begin()
    root_top_line.begin()
    line.begin()
    for i in range(KC):
        side_spread.begin(i, always)
    top_line.finish()
    for i in range(KC):
        top_spread.begin(i, always)
    for i in range(KC):
        top_spread.relay(i)
    for i in range(KC):
        side_spread.relay(i)
    for i in range(KC):
        top_spread.settle(i)
    line.relay()
    for i in range(KC):
        top_spread.finish(i)
    root_line.begin()
    root_top_line.finish()
    for i in range(KR):
        root_top_spread.begin(i, always)
    for i in range(KR):
        root_side_spread.begin(i, always)

    loads[1].wait()
    loads[3].wait()
    factor_top(KC, 0, top, cpiv, ctop)
    factor_top(KC, 1, top, cpiv, ctop)
    for i in range(KC):
        side_spread.settle(i)
    factor_top(KC, 2, top, cpiv, ctop)
    factor_top(KC, 3, top, cpiv, ctop)
    factor_top(KC, 4, top, cpiv, ctop)
    line.finish()
    for pair in range(KC // 2):
        factor_own(pair, down, cpiv, ctop, cown, mine)
    panels_store = pltpu.make_async_copy(cown, panels_out, store_sem.at[0])
    panels_store.start()
    root_line.relay()
    for i in range(KR):
        root_top_spread.relay(i)
    for i in range(KR):
        root_side_spread.relay(i)
    for i in range(KC):
        side_spread.finish(i)
    for pair in range(KC // 2):
        factor_wide(pair, side, cpiv, ctop, cside, 8 + col)

    def update_rows(t):
        rows = pl.ds(pl.multiple_of(t * B, B), B)
        product = dot_nn(cown[rows, :], cside[...])
        for s in range(CS):
            first = t * 8 * B + s + 1
            value = cwide[pl.ds(first, B, stride=8), :] - product[:, s * B:(s + 1) * B]
            update[t, :, s * B:(s + 1) * B] = value.astype(BF)

    partner = ((1 - child) * 2 + half, row, col)
    for p in range(2):
        t = 2 * p + 1 - child
        update_rows(t)
        traffic.send(always, update.at[t], came_out.at[p], u_send.at[p], u_recv.at[p], partner)
    keep_stores = []
    for p in range(2):
        t = 2 * p + child
        update_rows(t)
        keep_stores.append(pltpu.make_async_copy(update.at[t], keep_out.at[p], store_sem.at[1 + p]))
        keep_stores[-1].start()

    for i in range(KR):
        root_top_spread.settle(i)
    for i in range(KR):
        root_side_spread.settle(i)
    root_line.finish()
    for i in range(KR):
        root_top_spread.finish(i)
    for pair in range(KR // 2):
        factor_top(KR, pair, rtop, rpiv, xtop)
    for pair in range(KR // 2):
        factor_own(pair, rdown, rpiv, xtop, xown, root_class)
    root_panels_store = pltpu.make_async_copy(xown, root_panels_out, store_sem.at[3])
    root_panels_store.start()
    for i in range(KR):
        root_side_spread.finish(i)
    for pair in range(KR // 2):
        factor_wide(pair, rside, rpiv, xtop, xside, col)
    rest_stores = []
    for t in range(4):
        product = dot_nn(xown[t * B:(t + 1) * B, :], xside[...])
        for s in range(RS):
            place = pl.ds(t * RS * B + s, B, stride=RS)
            rwide[place, :] = rwide[place, :] - product[:, s * B:(s + 1) * B]
        block = pl.ds(t * RS * B, RS * B)
        rest_stores.append(pltpu.make_async_copy(rwide.at[block], rest_out.at[block], store_sem.at[4 + t]))
        rest_stores[-1].start()

    for p in range(2):
        traffic.landed(always, came_out.at[p], u_recv.at[p])
    traffic.drain()
    for store in [panels_store, root_panels_store] + keep_stores + rest_stores:
        store.wait()


def main_step(fronts, roots, child_pivots, root_pivots):
    dma = pltpu.SemaphoreType.DMA
    anywhere = pl.BlockSpec(memory_space=pl.ANY)
    return pl.pallas_call(
        main_kernel,
        out_shape=[
            jax.ShapeDtypeStruct((4 * B, KC * B), BF),
            jax.ShapeDtypeStruct((4 * B, KR * B), BF),
            jax.ShapeDtypeStruct((4 * B * RS, B), F32),
            jax.ShapeDtypeStruct((2, B, CS * B), BF),
            jax.ShapeDtypeStruct((2, B, CS * B), BF),
        ],
        in_specs=[anywhere] * 4,
        out_specs=[anywhere] * 5,
        scratch_shapes=[
            pltpu.VMEM((4, B, 8, B), BF),
            pltpu.VMEM((4, B, RS, B), BF),
            pltpu.VMEM((4 * B * 8, B), F32),
            pltpu.VMEM((4 * B * RS, B), F32),
            pltpu.VMEM((KC, B, B), F32),
            pltpu.VMEM((KR, B, B), F32),
            pltpu.VMEM((KC, KC, B, B), BF),
            pltpu.VMEM((KC, 4 * B, B), BF),
            pltpu.VMEM((KC, B, CS * B), BF),
            pltpu.VMEM((KR, KR, B, B), BF),
            pltpu.VMEM((KR, 4 * B, B), BF),
            pltpu.VMEM((KR, B, RS * B), BF),
            pltpu.VMEM((KC * B, KC * B), BF),
            pltpu.VMEM((4 * B, KC * B), BF),
            pltpu.VMEM((KC * B, CS * B), BF),
            pltpu.VMEM((KR * B, KR * B), BF),
            pltpu.VMEM((4 * B, KR * B), BF),
            pltpu.VMEM((KR * B, RS * B), BF),
            pltpu.VMEM((4, B, CS * B), BF),
            dma((4,)), dma((8,)),
            dma((2, 7)), dma((KC,)), dma((1, 7)), dma((KR,)),
            dma((2, 8)), dma((KC,)), dma((1, 8)), dma((KR,)),
            dma((KC, 8)), dma((2, KC)), dma((KC, 8)), dma((2, KC)),
            dma((KR, 8)), dma((2, KR)), dma((KR, 8)), dma((2, KR)),
            dma((2,)), dma((2,)),
        ],
        compiler_params=pltpu.CompilerParams(
            collective_id=0, has_side_effects=True, vmem_limit_bytes=56 * 2**20
        ),
        cost_estimate=pl.CostEstimate(flops=10**10, bytes_accessed=10**7, transcendentals=0),
    )(fronts, roots, child_pivots, root_pivots)


def add_kernel(maps, rest, keep, came, panels, root_panels, out, panels_out, root_panels_out, total, tiles, done, sems):
    child, half, row, col = position()
    passes = [
        pltpu.make_async_copy(panels, panels_out, sems.at[0]),
        pltpu.make_async_copy(root_panels, root_panels_out, sems.at[1]),
    ]
    fetch = [pltpu.make_async_copy(source, tiles.at[n], sems.at[2 + n]) for n, source in enumerate((keep, came))]
    height = RS * B
    blocks = [pl.ds(t * height, height) for t in range(4)]
    fetch += [pltpu.make_async_copy(rest.at[blocks[t]], total.at[blocks[t]], sems.at[4 + t]) for t in range(4)]
    for copy in fetch + passes:
        copy.start()
    for copy in fetch:
        copy.wait()
    for number, source in enumerate((child, 1 - child)):
        for p in range(2):
            i = (2 * p + child) * 16 + half * 8 + row - KC
            for s in range(1, 8):
                j = s * 8 + col - KC

                @pl.when((i >= 0) & (j >= 0))
                def _():
                    below = maps[source, jnp.maximum(i, 0)] // 32
                    across = maps[source, jnp.maximum(j, 0)] // 8
                    place = pl.ds(below * height + across, B, stride=RS)
                    total[place, :] = total[place, :] + tiles[number, p, :, (s - 1) * B:s * B].astype(F32)
    stores = []
    for t in range(4):
        for b in range(0, B, 32):
            at = (t * B + b) * RS
            done[t, b:b + 32] = total[at:at + 32 * RS, :].astype(BF).reshape(32, RS, B)
        stores.append(pltpu.make_async_copy(done.at[t], out.at[t], sems.at[8 + t]))
        stores[-1].start()
    for copy in stores + passes:
        copy.wait()


def add_step(maps, rest, keep, came, panels, root_panels):
    anywhere = pl.BlockSpec(memory_space=pl.ANY)
    return pl.pallas_call(
        add_kernel,
        out_shape=[
            jax.ShapeDtypeStruct((4, B, RS, B), BF),
            jax.ShapeDtypeStruct((4 * B, KC * B), BF),
            jax.ShapeDtypeStruct((4 * B, KR * B), BF),
        ],
        in_specs=[pl.BlockSpec(memory_space=pltpu.SMEM)] + [anywhere] * 5,
        out_specs=[anywhere] * 3,
        scratch_shapes=[
            pltpu.VMEM((4 * B * RS, B), F32),
            pltpu.VMEM((2, 2, B, CS * B), BF),
            pltpu.VMEM((4, B, RS, B), BF),
            pltpu.SemaphoreType.DMA((12,)),
        ],
        compiler_params=pltpu.CompilerParams(vmem_limit_bytes=48 * 2**20),
    )(maps, rest, keep, came, panels, root_panels)


def on_device(child_fronts, root_front, child_pivots, root_pivots, child_maps):
    fronts = child_fronts.reshape(4, B, 8, B)
    roots = root_front.reshape(4, B, RS, B)
    panels, root_panels, rest, keep, came = main_step(fronts, roots, child_pivots, root_pivots)
    root_rest, panels, root_panels = add_step(child_maps, rest, keep, came, panels, root_panels)
    return (
        panels.reshape(4, 1, B, KC * B),
        root_panels.reshape(4, 1, B, KR * B),
        root_rest.reshape(4, 1, B, RS, 1, B),
    )


def solution(mesh):
    placed = (
        P(None, ("cube", "row"), None, None, "col", None),
        P(None, ("cube", "row"), None, None, "col", None),
        P(),
        P(),
        P(),
    )
    return jax.shard_map(
        on_device,
        mesh=mesh,
        in_specs=placed,
        out_specs=(
            P(None, ("cube", "row"), None, None),
            P(None, ("cube", "row"), None, None),
            P(None, ("cube", "row"), None, None, "col", None),
        ),
        check_vma=False,
    )
```

time: 2430 us -> 104 us (0.04)
  the two profiles are of different devices: /device:TPU:25 before, /device:TPU:188 now
where the time goes in v2:
time: 104 us
  Pallas kernels  98.6 us (95%)
  local copies, waits for them, and re-layouts  4.39 us (4%)
    pallas_call x1, Pallas kernels, main_step(): pl.pallas_call(main_kernel, out_shape=[jax.ShapeDtypeStruct((4 * B, KC *...  91.6 us
    pallas_call x1, Pallas kernels, add_step(): pl.pallas_call(add_kernel, out_shape=[jax.ShapeDtypeStruct((4, B, RS, B),...  7.01 us
    unnamed x10, local copies, waits for them, and re-layouts  4.39 us

profile of v2, /device:TPU:188, one launch (start us, length us, event | category | flops | bytes accessed | tf_op | source)
XLA Modules:
  0.0 103.8 jit_solution(2432069176887787724)
XLA Ops:
  0.6 0.0 copy-start.4
  0.6 91.6 %shard_map.76 = (bf16[512,1280]{1,0:T(8,128)(2,1)}, bf16[512,512]{1,0:T(8,128)(2,1)}, f32[8192,128]{1,0:T(8,128)}, bf16[2,128,896]{2,1,0:T(8,128)(2,1)}, bf16[2,128,896]{2,1,0:T(8,128)(2,1)}) custom-call(bf16[4,128,8,128]{3,2,1,0:T(8,128)(2,1)} %bitcast.14, bf16[4,128,16,128]{3,2,1,0:T(8,128)(2,1)} %bitcast.11, f32[2,10,128,128]{3,2,1,0:T(8,128)} %child_pivots.1, ...), custom_call_target="tpu_custom_call" | custom-call | flops 10000000000 | bytes 10000000 | tf_op jit(solution)/shard_map/pallas_call | solution.py:481
  92.2 0.0 copy-done.4
  92.2 0.0 copy-start
  92.3 1.3 %copy-done = bf16[512,1280]{1,0:T(8,128)(2,1)S(1)} copy-done((bf16[512,1280]{1,0:T(8,128)(2,1)S(1)}, bf16[512,1280]{1,0:T(8,128)(2,1)}, u32[]{:S(2)}) %copy-start) | copy-done | bytes 1310744
  93.6 0.0 copy-start.1
  93.6 1.0 %copy-done.1 = bf16[512,512]{1,0:T(8,128)(2,1)S(1)} copy-done((bf16[512,512]{1,0:T(8,128)(2,1)S(1)}, bf16[512,512]{1,0:T(8,128)(2,1)}, u32[]{:S(2)}) %copy-start.1) | copy-done | bytes 524312
  94.6 0.0 copy-start.2
  94.6 1.0 copy-done.2
  95.6 0.0 copy-start.3
  95.6 1.0 copy-done.3
  96.6 7.0 %shard_map.77 = (bf16[4,128,16,128]{3,2,1,0:T(8,128)(2,1)}, bf16[512,1280]{1,0:T(8,128)(2,1)}, bf16[512,512]{1,0:T(8,128)(2,1)}) custom-call(s32[2,54]{1,0:T(2,128)S(1)} %copy-done.4, f32[8192,128]{1,0:T(8,128)} %get-tuple-element.11.rest, bf16[2,128,896]{2,1,0:T(8,128)(2,1)S(1)} %copy-done.2, bf16[2,128,896]{2,1,0:T(8,128)(2,1)S(1)} %copy-done.3, ...), custom_call_target="tpu_custom_call" | custom-call | tf_op jit(solution)/shard_map/pallas_call | solution.py:565
Async XLA Ops:
  0.6 91.6 %copy-start.4 = (s32[2,54]{1,0:T(2,128)S(1)}, s32[2,54]{1,0:T(2,128)}, u32[]{:S(2)}) copy-start(s32[2,54]{1,0:T(2,128)} %maps.1) | copy-start | bytes 1300
  92.2 1.3 %copy-start = (bf16[512,1280]{1,0:T(8,128)(2,1)S(1)}, bf16[512,1280]{1,0:T(8,128)(2,1)}, u32[]{:S(2)}) copy-start(bf16[512,1280]{1,0:T(8,128)(2,1)} %get-tuple-element.14.panels) | copy-start | bytes 3932164
  93.6 1.0 %copy-start.1 = (bf16[512,512]{1,0:T(8,128)(2,1)S(1)}, bf16[512,512]{1,0:T(8,128)(2,1)}, u32[]{:S(2)}) copy-start(bf16[512,512]{1,0:T(8,128)(2,1)} %get-tuple-element.15.root_panels) | copy-start | bytes 1572868
  94.6 1.0 copy-start.2
  95.6 1.0 copy-start.3

commit v3 on v2

v3 whole, which is shorter than its diff:
```python
import functools

import jax
import jax.numpy as jnp
from jax import lax
from jax.experimental import pallas as pl
from jax.experimental.pallas import tpu as pltpu
from jax.sharding import PartitionSpec as P

B = 128
KC = 10
KR = 4
CS = 7
RS = 16
MESH = pl.DeviceIdType.MESH
BF = jnp.bfloat16
F32 = jnp.float32


def dot_nn(left, right):
    return lax.dot_general(left, right, (((1,), (0,)), ((), ())), preferred_element_type=F32)


def dot_nt(left, right):
    return lax.dot_general(left, right, (((1,), (1,)), ((), ())), preferred_element_type=F32)


def split(value):
    high = value.astype(BF)
    return high, (value - high.astype(F32)).astype(BF)


def times_pivot(value, pivot):
    pivot_high, pivot_low = split(pivot)
    upper = jnp.concatenate([pivot_high, pivot_low], axis=1)
    lower = jnp.concatenate([pivot_high, jnp.zeros_like(pivot_low)], axis=1)
    product = dot_nn(jnp.concatenate(split(value), axis=1), jnp.concatenate([upper, lower], axis=0))
    return product[:, :B] + product[:, B:]


def pivot_times(pivot_t, value):
    pivot_high, pivot_low = split(pivot_t)
    upper = jnp.concatenate([pivot_high, pivot_high], axis=1)
    lower = jnp.concatenate([pivot_low, jnp.zeros_like(pivot_low)], axis=1)
    product = dot_nn(jnp.concatenate([upper, lower], axis=0), jnp.concatenate(split(value), axis=0))
    return product[:B] + product[B:]


def position():
    cube = lax.axis_index("cube")
    return cube // 2, cube % 2, lax.axis_index("row"), lax.axis_index("col")


class Starter:
    def __init__(self, number=0):
        self.number = number

    def send(self, source, target, send_sem, recv_sem, device):
        remote(source, target, send_sem, recv_sem, device).start()

    def landed(self, block, recv_sem):
        child, half, row, col = position()
        remote(block, block, recv_sem, recv_sem, (child * 2 + 1 - half, row, col)).wait_recv()


class Drainer:
    def __init__(self, number=0):
        self.number = number

    def send(self, source, target, send_sem, recv_sem, device):
        remote(source, target, send_sem, recv_sem, device).wait_send()

    def landed(self, block, recv_sem):
        pass


def remote(source, target, send_sem, recv_sem, device):
    return pltpu.make_async_remote_copy(
        src_ref=source, dst_ref=target, send_sem=send_sem, recv_sem=recv_sem,
        device_id=device, device_id_type=MESH,
    )


class Traffic:
    def __init__(self):
        self.pending = []

    def starter(self):
        return Starter()

    def run(self, cond, body, number=0):
        op = Starter(number)
        pl.when(cond)(lambda: body(op))
        self.pending.append((cond, body, number))
        return op.number

    def drain(self):
        for cond, body, number in self.pending:
            pl.when(cond)(lambda: body(Drainer(number)))
        self.pending = []


class PairSpread:
    def __init__(self, traffic, buffer, size, hand, recv, sems):
        self.traffic, self.buffer, self.size, self.hand = traffic, buffer, size, hand
        self.recv, self.sems, self.number = recv, sems, 0
        child, half, row, col = position()
        self.half, self.row, self.x, self.y = half, row, row // 2, row % 2
        self.sibling = (child * 2 + 1 - half, row, col)
        self.plus, self.minus = [(child * 2 + half, (self.x + d) % 4 * 2 + self.y, col) for d in (1, 3)]
        self.across = (child * 2 + half, row + 1 - 2 * self.y, col)
        self.mine = half * 8 + row
        self.other = (1 - half) * 8 + row

    def part(self, slot, half):
        if self.size is None:
            return self.buffer.at[slot], self.recv.at[0, slot]
        start = pl.multiple_of(half * self.size, self.size)
        return self.buffer.at[slot, pl.ds(start, self.size)], self.recv.at[half, slot]

    def _send(self, op, slot, device, half=None):
        block, recv = self.part(slot, self.half if half is None else half)
        op.send(block, block, self.sems.at[op.number], recv, device)
        op.number += 1

    def _wait(self, op, slot, half=None):
        block, recv = self.part(slot, self.half if half is None else half)
        op.landed(block, recv)

    def _pass(self, op, slot):
        if self.size is not None:
            self._send(op, slot, self.sibling)

    def _run(self, cond, body):
        self.number = self.traffic.run(cond, body, self.number)

    def _each(self, chips, body):
        for chip in chips:
            body(chip)
            pl.when(chip < 2)(lambda: body(8 + chip % 2))

    def _row(self, d, e):
        return (self.x + d) % 4 * 2 + (self.y + e) % 2

    def begin(self):
        def own(op):
            slot = self.mine % KC
            if self.size is None:
                block, recv = self.part(slot, self.half)
                op.send(self.hand, block, self.sems.at[op.number], recv, self.sibling)
                op.number += 1
            else:
                self._send(op, slot, self.sibling, 1 - self.half)
            for device in (self.across, self.plus, self.minus):
                self._send(op, slot, device)
            self._pass(op, slot)

        def others(op):
            slot = self.other % KC
            self._wait(op, slot)
            for device in (self.across, self.plus, self.minus):
                self._send(op, slot, device)

        self._run(self.mine < KC, own)
        self._run(self.other < KC, others)

    def _onward(self, op, slot, d):
        if d == 3:
            pl.when(slot < 4)(lambda: self._send(op, slot, self.plus))
        else:
            pl.when(slot >= 4)(lambda: self._send(op, slot, self.minus))

    def relay(self):
        def first(op):
            for d in (3, 1):
                def body(slot):
                    self._wait(op, slot)
                    self._onward(op, slot, d)
                    self._send(op, slot, self.across)
                    self._pass(op, slot)

                self._each([self._row(d, 0)], body)

        def second(op):
            def body(slot):
                self._wait(op, slot)
                self._send(op, slot, self.plus)
                self._send(op, slot, self.minus)
                self._pass(op, slot)

            self._each([self._row(0, 1)], body)

        self._run(self.half == 0, first)
        self._run(self.half == 1, second)

    def relay2(self):
        def first(op):
            def body(slot):
                self._wait(op, slot)
                self._send(op, slot, self.across)
                self._pass(op, slot)

            self._each([self._row(2, 0)], body)

        def second(op):
            for e in range(2):
                for d in (3, 1):
                    def body(slot):
                        self._wait(op, slot)
                        self._onward(op, slot, d)
                        self._pass(op, slot)

                    self._each([self._row(d, e)], body)

        self._run(self.half == 0, first)
        self._run(self.half == 1, second)

    def settle(self):
        def body(op, slot):
            self._wait(op, slot)
            self._pass(op, slot)

        def first(op):
            self._each([self._row(d, 1) for d in (0, 3, 1, 2)], lambda slot: body(op, slot))

        def second(op):
            self._each([self._row(2, e) for e in range(2)], lambda slot: body(op, slot))

        self._run(self.half == 0, first)
        self._run(self.half == 1, second)

    def finish(self):
        if self.size is None:
            return
        op = self.traffic.starter()
        pl.when(self.other < KC)(lambda: self._wait(op, self.other % KC, 1 - self.half))
        chips = [self._row(d, e) for d in range(4) for e in range(2)][1:]
        self._each(chips, lambda slot: self._wait(op, slot, 1 - self.half))


class PlaneShare:
    def __init__(self, traffic, buffer, hand, recv, sems):
        self.traffic, self.buffer, self.hand, self.recv, self.sems, self.number = traffic, buffer, hand, recv, sems, 0
        child, half, row, col = position()
        self.half = half
        self.sibling = (child * 2 + 1 - half, row, col)
        x, y = row // 2, child * 2 + row % 2

        def device(dx, dy):
            place = (y + dy) % 4
            return (place // 2 * 2 + half, (x + dx) % 4 * 2 + place % 2, col)

        def either(first, second):
            return tuple(jnp.where(half == 0, one, two) for one, two in zip(first, second))

        self.first = [either(device(d, 0), device(0, d)) for d in (1, 3)]
        self.second = [either(device(0, d), device(d, 0)) for d in (1, 3)]
        self.slots = []
        for i in range(KR):
            begin_1 = jnp.where(half == 0, i // 2, i % 2)
            begin_2 = jnp.where(half == 0, i % 2, i // 2)
            far_1 = (jnp.where(half == 0, x, y) - begin_1 + 4) % 4
            far_2 = (jnp.where(half == 0, y, x) - begin_2 + 4) % 4
            self.slots.append((i, begin_1, begin_2, far_1, far_2))

    def _send(self, op, i, device):
        block = self.buffer.at[i]
        op.send(block, block, self.sems.at[op.number], self.recv.at[i], device)
        op.number += 1

    def _wait(self, op, i):
        op.landed(self.buffer.at[i], self.recv.at[i])

    def _run(self, cond, body):
        self.number = self.traffic.run(cond, body, self.number)

    def _onward(self, op, i, begin, far, devices):
        pl.when((begin == 1) & (far == 1))(lambda: self._send(op, i, devices[0]))
        pl.when((begin == 0) & (far == 3))(lambda: self._send(op, i, devices[1]))

    def begin(self):
        for i, begin_1, begin_2, far_1, far_2 in self.slots:
            chip = (far_1 == 0) & (far_2 == 0)

            def body(op, i=i):
                @pl.when(self.half == 0)
                def _():
                    hand = self.buffer.at[i] if self.hand is None else self.hand
                    op.send(hand, self.buffer.at[i], self.sems.at[op.number], self.recv.at[i], self.sibling)

                op.number += 1
                pl.when(self.half == 1)(lambda: self._wait(op, i))
                for device in self.first + self.second:
                    self._send(op, i, device)

            self._run(chip, body)

    def relay(self):
        for i, begin_1, begin_2, far_1, far_2 in self.slots:
            def body(op, i=i, begin_1=begin_1, far_1=far_1):
                self._wait(op, i)
                self._onward(op, i, begin_1, far_1, self.first)
                for device in self.second:
                    self._send(op, i, device)

            self._run((far_2 == 0) & (far_1 % 2 == 1), body)

    def relay2(self):
        for i, begin_1, begin_2, far_1, far_2 in self.slots:
            def body(op, i=i):
                self._wait(op, i)
                for device in self.second:
                    self._send(op, i, device)

            self._run((far_2 == 0) & (far_1 == 2), body)

    def relay3(self):
        for i, begin_1, begin_2, far_1, far_2 in self.slots:
            def body(op, i=i, begin_2=begin_2, far_2=far_2):
                self._wait(op, i)
                self._onward(op, i, begin_2, far_2, self.second)

            self._run(far_2 % 2 == 1, body)

    def finish(self):
        op = self.traffic.starter()
        for i, begin_1, begin_2, far_1, far_2 in self.slots:
            pl.when(far_2 == 2)(lambda: self._wait(op, i))


class Line:
    def __init__(self, traffic, buffer, count, recv, sems):
        self.traffic, self.buffer, self.count, self.recv, self.sems = traffic, buffer, count, recv, sems
        child, half, row, col = position()
        self.col = col
        self.places = [(child * 2 + half, row, (col + d) % 8) for d in (1, 7)]

    def _each(self, step, body):
        base = (self.col + step + 8) % 8
        for extra in range((self.count + 7) // 8):
            limit = min(self.count - 8 * extra, 8)

            def run(op, extra=extra, limit=limit):
                body(op, extra, 8 * extra + base % limit)

            self.traffic.run(base < limit, run)

    def begin(self):
        def body(op, extra, slot):
            block = self.buffer.at[slot]
            for way in range(2):
                op.send(block, block, self.sems.at[extra, way], self.recv.at[0, slot], self.places[way])

        self._each(0, body)

    def relay(self, step):
        for way in range(2):
            def body(op, extra, slot, way=way):
                block = self.buffer.at[slot]
                op.landed(block, self.recv.at[0, slot])
                number = 0
                if step == 3:
                    block = self.buffer.at[slot, pl.ds(way * 2 * B, 2 * B)]
                    number = way
                op.send(
                    block, block, self.sems.at[extra, 2 * step + way], self.recv.at[number, slot], self.places[way]
                )

            self._each(step if way else -step, body)

    def finish(self):
        def body(op, extra, slot):
            for way in range(2):
                op.landed(self.buffer.at[slot, pl.ds(way * 2 * B, 2 * B)], self.recv.at[way, slot])

        self._each(4, body)


class TopLine:
    def __init__(self, traffic, count, buffer, recv, sems, owns, mine):
        child, half, row, col = position()
        self.traffic, self.count, self.buffer, self.recv, self.sems = traffic, count, buffer, recv, sems
        self.owns, self.mine, self.col = owns, mine % count, col
        self.depth = count // 2 + 1
        self.places = [(child * 2 + half, row, (col + d) % 8) for d in (1, 7, 2, 6, 3, 5, 4)]

    def held(self):
        for extra in range((self.count + 7) // 8):
            limit = min(self.count - 8 * extra, 8)
            index = 8 * extra + self.col % limit
            place = (index - self.mine + self.count) % self.count
            yield extra, self.owns & (self.col < limit) & (place < self.depth), index, place % self.depth

    def begin(self):
        for extra, cond, index, place in self.held():
            def body(op, extra=extra, index=index, place=place):
                block = self.buffer.at[self.mine, place]
                for n, device in enumerate(self.places):
                    op.send(block, block, self.sems.at[extra, n], self.recv.at[index], device)

            self.traffic.run(cond, body)

    def finish(self):
        op = self.traffic.starter()

        @pl.when(self.owns)
        def _():
            for place in range(self.depth):
                index = (self.mine + place) % self.count

                @pl.when(index % 8 != self.col)
                def _():
                    op.landed(self.buffer.at[self.mine, place], self.recv.at[index])


def greet_all():
    child, half, row, col = position()
    cube = child * 2 + half
    x, y = row // 2, child * 2 + row % 2
    barrier = pltpu.get_barrier_semaphore()
    others = [(cube, row, (col + d) % 8) for d in range(1, 8)]
    others += [(cube, (x + d) % 4 * 2 + row % 2, col) for d in range(1, 4)]
    others += [((y + d) % 4 // 2 * 2 + half, x * 2 + (y + d) % 2, col) for d in range(1, 4)]
    others += [(child * 2 + 1 - half, row, col)]
    for device in others:
        pl.semaphore_signal(barrier, inc=1, device_id=device, device_id_type=MESH)
    return barrier, len(others)


def top_tile(count, top, i, k):
    place = (k - i) % count
    if place <= count // 2:
        return top[i, place].astype(F32)
    return top[k, (i - k) % count].astype(F32).T


def factor_top(count, pair, top, pivots, panels):
    k = 2 * pair
    at = k * B
    first = jnp.concatenate([top_tile(count, top, i, k) for i in range(k, count)], axis=0)
    second = jnp.concatenate([top_tile(count, top, i, k + 1) for i in range(k + 1, count)], axis=0)
    if pair:
        both = dot_nt(panels[at:, :at], panels[at:at + 2 * B, :at])
        first = first - both[:, :B]
        second = second - both[B:, B:]
    first = times_pivot(first, pivots[k]).astype(BF)
    panels[at:, at:at + B] = first
    second = second - dot_nt(first[B:], first[B:2 * B])
    panels[at + B:, at + B:at + 2 * B] = times_pivot(second, pivots[k + 1]).astype(BF)


def factor_own(pair, down, pivots, panels_top, panels, row_class, rows, first_block):
    k = 2 * pair
    at = k * B
    length = rows.stop - rows.start
    block = (lax.broadcasted_iota(jnp.int32, (length, B), 0) + rows.start) // B
    row_block = block == first_block
    first = down[k, rows].astype(F32)
    second = down[k + 1, rows].astype(F32)
    if pair:
        both = dot_nt(panels[rows, :at], panels_top[at:at + 2 * B, :at])
        first = first - both[:, :B]
        second = second - both[:, B:]
    first = times_pivot(first, pivots[k])
    first = jnp.where(row_block & (row_class < k), 0.0, first).astype(BF)
    panels[rows, at:at + B] = first
    second = second - dot_nt(first, panels_top[at + B:at + 2 * B, at:at + B])
    second = times_pivot(second, pivots[k + 1])
    second = jnp.where(row_block & (row_class < k + 1), 0.0, second).astype(BF)
    panels[rows, at + B:at + 2 * B] = second


def factor_wide(pair, side, pivots, panels_top, wide, first_tile):
    k = 2 * pair
    at = k * B
    col_block = lax.broadcasted_iota(jnp.int32, (B, wide.shape[1]), 1) < B
    first = side[k].astype(F32)
    second = side[k + 1].astype(F32)
    if pair:
        both = dot_nn(panels_top[at:at + 2 * B, :at], wide[:at, :])
        first = first - both[:B]
        second = second - both[B:]
    first = pivot_times(pivots[k].T, first)
    first = jnp.where(col_block & (first_tile < k), 0.0, first).astype(BF)
    wide[at:at + B, :] = first
    second = second - dot_nn(panels_top[at + B:at + 2 * B, at:at + B], first)
    second = pivot_times(pivots[k + 1].T, second)
    second = jnp.where(col_block & (first_tile < k + 1), 0.0, second).astype(BF)
    wide[at + B:at + 2 * B, :] = second


def main_kernel(
    fronts, roots, child_pivots, root_pivots,
    panels_out, root_panels_out, rest_out, keep_out, came_out,
    craw, rraw, cwide, rwide, cpiv, rpiv,
    top, down, side, rtop, rdown, rside,
    hand, rhand, ctop, cown, cside, cother, xtop, xown, xside, xother, update,
    load_sem, store_sem, tl_send, tl_recv, rtl_send, rtl_recv, line_send, line_recv, rline_send, rline_recv,
    t_send, t_recv, s_send, s_recv, rt_send, rt_recv, rs_send, rs_recv, u_send, u_recv,
    q_send, q_recv, rq_send, rq_recv,
):
    child, half, row, col = position()
    mine = half * 8 + row
    root_class = child * 16 + mine
    owns = mine < KC
    root_owns = (child == 0) & (half == 0) & (row < KR)

    loads = [
        pltpu.make_async_copy(fronts, craw, load_sem.at[0]),
        pltpu.make_async_copy(child_pivots.at[child], cpiv, load_sem.at[1]),
        pltpu.make_async_copy(roots, rraw, load_sem.at[2]),
        pltpu.make_async_copy(root_pivots, rpiv, load_sem.at[3]),
    ]
    for load in loads:
        load.start()
    barrier, count = greet_all()

    traffic = Traffic()
    top_line = TopLine(traffic, KC, top, tl_recv, tl_send, owns, mine)
    root_top_line = TopLine(traffic, KR, rtop, rtl_recv, rtl_send, root_owns, row)
    line = Line(traffic, down, KC, line_recv, line_send)
    root_line = Line(traffic, rdown, KR, rline_recv, rline_send)
    top_spread = PairSpread(traffic, top, 3, None, t_recv, t_send)
    side_spread = PairSpread(traffic, side, None, hand, s_recv, s_send)
    root_top_spread = PlaneShare(traffic, rtop, None, rt_recv, rt_send)
    root_side_spread = PlaneShare(traffic, rside, rhand, rs_recv, rs_send)
    always = col >= 0

    loads[0].wait()
    for t in range(4):
        cwide[t * 8 * B:(t + 1) * 8 * B, :] = craw[t].astype(F32).reshape(8 * B, B)

    order = [1 - child, 3 - child, child, 2 + child]

    def place_column(line_buffer, count, line_top, wide, stride, order):
        for extra, cond, index, place in line_top.held():
            @pl.when((col + 8 * extra) < count)
            def _():
                for n, t in enumerate(order):
                    column = wide[pl.ds(t * B * stride + extra, B, stride=stride), :]
                    line_buffer[index, n * B:(n + 1) * B] = column.astype(BF)

                @pl.when(cond)
                def _():
                    line_top.buffer[line_top.mine, place] = wide[pl.ds(extra, B, stride=stride), :].astype(BF)

    place_column(down, KC, top_line, cwide, 8, order)
    own_first = 1 + 3 * half
    other_first = 5 - 4 * half

    @pl.when(owns)
    def _():
        for s in range(4):
            columns = slice(s * B, (s + 1) * B)
            side[mine % KC, :, columns] = cwide[pl.ds(own_first + s, B, stride=8), :].astype(BF)
            hand[:, columns] = cwide[pl.ds(4 - 3 * half + s, B, stride=8), :].astype(BF)

    pl.semaphore_wait(barrier, count)
    top_line.begin()
    line.begin()
    side_spread.begin()

    loads[2].wait()
    for t in range(4):
        for b in range(0, B, 32):
            at = (t * B + b) * RS
            rwide[at:at + 32 * RS, :] = rraw[t, b:b + 32].astype(F32).reshape(32 * RS, B)
    place_column(rdown, KR, root_top_line, rwide, RS, range(4))

    @pl.when(root_owns)
    def _():
        for s in range(8):
            columns = slice(s * B, (s + 1) * B)
            rside[row % KR, :, columns] = rwide[pl.ds(s, B, stride=RS), :].astype(BF)
            rhand[:, columns] = rwide[pl.ds(8 + s, B, stride=RS), :].astype(BF)

    root_top_line.begin()
    top_line.finish()
    top_spread.begin()
    line.relay(1)
    top_spread.relay()
    side_spread.relay()
    line.relay(2)
    top_spread.relay2()
    root_top_line.finish()
    root_top_spread.begin()
    root_side_spread.begin()
    side_spread.relay2()
    top_spread.settle()
    line.relay(3)
    root_line.begin()
    top_spread.finish()

    loads[1].wait()
    loads[3].wait()
    for pair in range(2):
        factor_top(KC, pair, top, cpiv, ctop)
    root_top_spread.relay()
    root_side_spread.relay()
    for pair in range(2, 4):
        factor_top(KC, pair, top, cpiv, ctop)
    root_top_spread.relay2()
    root_side_spread.relay2()
    root_line.relay(1)
    factor_top(KC, 4, top, cpiv, ctop)
    line.finish()
    side_spread.settle()

    sibling = (child * 2 + 1 - half, row, col)
    partner = ((1 - child) * 2 + half, row, col)
    first_block = jnp.where(child == 1, 0, 2)

    def to_sibling(buffer, other, pair, send_sem, recv_sem):
        block = pl.ds(2 * pair * B, 2 * B)

        def body(op):
            op.send(buffer.at[block], other.at[block], send_sem.at[pair], recv_sem.at[pair], sibling)

        traffic.run(always, body)

    def from_sibling(other, pair, recv_sem):
        Starter().landed(other.at[pl.ds(2 * pair * B, 2 * B)], recv_sem.at[pair])

    def update_own(n):
        product = dot_nn(cown[n * B:(n + 1) * B, :], cside[...])
        for s in range(4):
            value = cwide[pl.ds(order[n] * 8 * B + own_first + s, B, stride=8), :]
            update[n, :, s * B:(s + 1) * B] = (value - product[:, s * B:(s + 1) * B]).astype(BF)

    def update_other(n):
        columns = pl.ds(pl.multiple_of((1 - half) * B, B), 3 * B)
        product = dot_nn(cown[n * B:(n + 1) * B, :], cother[:, columns])
        for s in range(3):
            value = cwide[pl.ds(order[n] * 8 * B + other_first + s, B, stride=8), :]
            update[n, :, (4 + s) * B:(5 + s) * B] = (value - product[:, s * B:(s + 1) * B]).astype(BF)

    def send_update(n, part):
        columns = pl.ds(0, 4 * B) if part == 0 else pl.ds(4 * B, 3 * B)

        def body(op):
            op.send(
                update.at[n, :, columns], came_out.at[n, :, columns],
                u_send.at[part, n], u_recv.at[part, n], partner,
            )

        traffic.run(always, body)

    for pair in range(KC // 2):
        factor_wide(pair, side, cpiv, ctop, cside, 8 + 24 * half + col)
        factor_own(pair, down, cpiv, ctop, cown, mine, slice(0, 2 * B), first_block)
        to_sibling(cside, cother, pair, q_send, q_recv)
    root_top_spread.relay3()
    root_side_spread.relay3()
    for n in range(2):
        update_own(n)
        send_update(n, 0)
    for pair in range(KC // 2):
        from_sibling(cother, pair, q_recv)
    for n in range(2):
        update_other(n)
        send_update(n, 1)
    root_line.relay(2)
    for pair in range(KC // 2):
        factor_own(pair, down, cpiv, ctop, cown, mine, slice(2 * B, 4 * B), first_block)
    panels_stores = []
    for n in range(4):
        rows = pl.ds(pl.multiple_of(order[n] * B, B), B)
        panels_stores.append(
            pltpu.make_async_copy(cown.at[pl.ds(n * B, B)], panels_out.at[rows], store_sem.at[8 + n])
        )
        panels_stores[-1].start()
    for n in range(2, 4):
        update_own(n)
        update_other(n)
    keep_store = pltpu.make_async_copy(update.at[pl.ds(2, 2)], keep_out, store_sem.at[0])
    keep_store.start()
    root_line.relay(3)

    root_top_spread.finish()
    for pair in range(KR // 2):
        factor_top(KR, pair, rtop, rpiv, xtop)
    root_side_spread.finish()
    for pair in range(KR // 2):
        factor_wide(pair, rside, rpiv, xtop, xside, 64 * half + col)
        to_sibling(xside, xother, pair, rq_send, rq_recv)
    root_line.finish()
    for pair in range(KR // 2):
        factor_own(pair, rdown, rpiv, xtop, xown, root_class, slice(0, 4 * B), 0)
    root_panels_store = pltpu.make_async_copy(xown, root_panels_out, store_sem.at[3])
    root_panels_store.start()
    for pair in range(KR // 2):
        from_sibling(xother, pair, rq_recv)
    rest_stores = []
    for t in range(4):
        for buffer, first in ((xside, 8 * half), (xother, 8 - 8 * half)):
            product = dot_nn(xown[t * B:(t + 1) * B, :], buffer[...])
            for s in range(8):
                place = pl.ds(t * RS * B + first + s, B, stride=RS)
                rwide[place, :] = rwide[place, :] - product[:, s * B:(s + 1) * B]
        block = pl.ds(t * RS * B, RS * B)
        rest_stores.append(pltpu.make_async_copy(rwide.at[block], rest_out.at[block], store_sem.at[4 + t]))
        rest_stores[-1].start()

    for n in range(2):
        Starter().landed(came_out.at[n, :, pl.ds(0, 4 * B)], u_recv.at[0, n])
        Starter().landed(came_out.at[n, :, pl.ds(4 * B, 3 * B)], u_recv.at[1, n])
    traffic.drain()
    for store in [keep_store, root_panels_store] + panels_stores + rest_stores:
        store.wait()


def main_step(fronts, roots, child_pivots, root_pivots):
    dma = pltpu.SemaphoreType.DMA
    anywhere = pl.BlockSpec(memory_space=pltpu.HBM)
    return pl.pallas_call(
        main_kernel,
        out_shape=[
            jax.ShapeDtypeStruct((4 * B, KC * B), BF),
            jax.ShapeDtypeStruct((4 * B, KR * B), BF),
            jax.ShapeDtypeStruct((4 * B * RS, B), F32),
            jax.ShapeDtypeStruct((2, B, CS * B), BF),
            jax.ShapeDtypeStruct((2, B, CS * B), BF),
        ],
        in_specs=[anywhere] * 4,
        out_specs=[anywhere] * 5,
        scratch_shapes=[
            pltpu.VMEM((4, B, 8, B), BF),
            pltpu.VMEM((4, B, RS, B), BF),
            pltpu.VMEM((4 * B * 8, B), F32),
            pltpu.VMEM((4 * B * RS, B), F32),
            pltpu.VMEM((KC, B, B), F32),
            pltpu.VMEM((KR, B, B), F32),
            pltpu.VMEM((KC, KC // 2 + 1, B, B), BF),
            pltpu.VMEM((KC, 4 * B, B), BF),
            pltpu.VMEM((KC, B, 4 * B), BF),
            pltpu.VMEM((KR, KR // 2 + 1, B, B), BF),
            pltpu.VMEM((KR, 4 * B, B), BF),
            pltpu.VMEM((KR, B, 8 * B), BF),
            pltpu.VMEM((B, 4 * B), BF),
            pltpu.VMEM((B, 8 * B), BF),
            pltpu.VMEM((KC * B, KC * B), BF),
            pltpu.VMEM((4 * B, KC * B), BF),
            pltpu.VMEM((KC * B, 4 * B), BF),
            pltpu.VMEM((KC * B, 4 * B), BF),
            pltpu.VMEM((KR * B, KR * B), BF),
            pltpu.VMEM((4 * B, KR * B), BF),
            pltpu.VMEM((KR * B, 8 * B), BF),
            pltpu.VMEM((KR * B, 8 * B), BF),
            pltpu.VMEM((4, B, CS * B), BF),
            dma((4,)), dma((12,)),
            dma((2, 7)), dma((KC,)), dma((1, 7)), dma((KR,)),
            dma((2, 8)), dma((2, KC)), dma((1, 8)), dma((2, KR)),
            dma((64,)), dma((2, KC)), dma((64,)), dma((1, KC)),
            dma((64,)), dma((KR,)), dma((64,)), dma((KR,)),
            dma((2, 2)), dma((2, 2)), dma((5,)), dma((5,)), dma((2,)), dma((2,)),
        ],
        compiler_params=pltpu.CompilerParams(
            collective_id=0, has_side_effects=True, vmem_limit_bytes=56 * 2**20
        ),
        cost_estimate=pl.CostEstimate(flops=10**10, bytes_accessed=10**7, transcendentals=0),
    )(fronts, roots, child_pivots, root_pivots)


def add_kernel(maps, rest, keep, came, panels, root_panels, out, panels_out, root_panels_out, total, tiles, done, sems):
    child, half, row, col = position()
    passes = [
        pltpu.make_async_copy(panels, panels_out, sems.at[0]),
        pltpu.make_async_copy(root_panels, root_panels_out, sems.at[1]),
    ]
    fetch = [pltpu.make_async_copy(source, tiles.at[n], sems.at[2 + n]) for n, source in enumerate((keep, came))]
    height = RS * B
    blocks = [pl.ds(t * height, height) for t in range(4)]
    fetch += [pltpu.make_async_copy(rest.at[blocks[t]], total.at[blocks[t]], sems.at[4 + t]) for t in range(4)]
    for copy in fetch + passes:
        copy.start()
    for copy in fetch:
        copy.wait()
    for number, source in enumerate((child, 1 - child)):
        for p in range(2):
            i = (2 * p + child) * 16 + half * 8 + row - KC
            for n in range(7):
                s = 1 + 3 * half + n if n < 4 else 1 - 4 * half + n
                j = s * 8 + col - KC

                @pl.when((i >= 0) & (j >= 0))
                def _():
                    below = maps[source, jnp.maximum(i, 0)] // 32
                    across = maps[source, jnp.maximum(j, 0)] // 8
                    place = pl.ds(below * height + across, B, stride=RS)
                    total[place, :] = total[place, :] + tiles[number, p, :, n * B:(n + 1) * B].astype(F32)
    stores = []
    for t in range(4):
        for b in range(0, B, 32):
            at = (t * B + b) * RS
            done[t, b:b + 32] = total[at:at + 32 * RS, :].astype(BF).reshape(32, RS, B)
        stores.append(pltpu.make_async_copy(done.at[t], out.at[t], sems.at[8 + t]))
        stores[-1].start()
    for copy in stores + passes:
        copy.wait()


def add_step(maps, rest, keep, came, panels, root_panels):
    anywhere = pl.BlockSpec(memory_space=pltpu.HBM)
    return pl.pallas_call(
        add_kernel,
        out_shape=[
            jax.ShapeDtypeStruct((4, B, RS, B), BF),
            jax.ShapeDtypeStruct((4 * B, KC * B), BF),
            jax.ShapeDtypeStruct((4 * B, KR * B), BF),
        ],
        in_specs=[pl.BlockSpec(memory_space=pltpu.SMEM)] + [anywhere] * 5,
        out_specs=[anywhere] * 3,
        scratch_shapes=[
            pltpu.VMEM((4 * B * RS, B), F32),
            pltpu.VMEM((2, 2, B, CS * B), BF),
            pltpu.VMEM((4, B, RS, B), BF),
            pltpu.SemaphoreType.DMA((12,)),
        ],
        compiler_params=pltpu.CompilerParams(vmem_limit_bytes=48 * 2**20),
    )(maps, rest, keep, came, panels, root_panels)


def on_device(child_fronts, root_front, child_pivots, root_pivots, child_maps):
    fronts = child_fronts.reshape(4, B, 8, B)
    roots = root_front.reshape(4, B, RS, B)
    panels, root_panels, rest, keep, came = main_step(fronts, roots, child_pivots, root_pivots)
    root_rest, panels, root_panels = add_step(child_maps, rest, keep, came, panels, root_panels)
    return (
        panels.reshape(4, 1, B, KC * B),
        root_panels.reshape(4, 1, B, KR * B),
        root_rest.reshape(4, 1, B, RS, 1, B),
    )


def solution(mesh):
    placed = (
        P(None, ("cube", "row"), None, None, "col", None),
        P(None, ("cube", "row"), None, None, "col", None),
        P(),
        P(),
        P(),
    )
    return jax.shard_map(
        on_device,
        mesh=mesh,
        in_specs=placed,
        out_specs=(
            P(None, ("cube", "row"), None, None),
            P(None, ("cube", "row"), None, None),
            P(None, ("cube", "row"), None, None, "col", None),
        ),
        check_vma=False,
    )
```

time: 104 us -> 85 us (0.82)
  the two profiles are of different devices: /device:TPU:188 before, /device:TPU:25 now
where the time goes in v3:
time: 85 us; the launch traced here: 84.7 us
  Pallas kernels  79.5 us (94%)
  local copies, waits for them, and re-layouts  4.39 us (5%)
  between operations  0.85 us (1%)
    pallas_call x1, Pallas kernels, main_step(): pl.pallas_call(main_kernel, out_shape=[jax.ShapeDtypeStruct((4 * B, KC *...  72.6 us
    pallas_call x1, Pallas kernels, add_step(): pl.pallas_call(add_kernel, out_shape=[jax.ShapeDtypeStruct((4, B, RS, B),...  6.86 us
    unnamed x10, local copies, waits for them, and re-layouts  4.39 us

profile of v3, /device:TPU:25, one launch (start us, length us, event | category | flops | bytes accessed | tf_op | source)
XLA Modules:
  0.0 84.7 jit_solution(6615120450909516370)
XLA Ops:
  0.6 0.0 copy-start.4
  0.6 72.6 %shard_map.76 = (bf16[512,1280]{1,0:T(8,128)(2,1)}, bf16[512,512]{1,0:T(8,128)(2,1)}, f32[8192,128]{1,0:T(8,128)}, bf16[2,128,896]{2,1,0:T(8,128)(2,1)}, bf16[2,128,896]{2,1,0:T(8,128)(2,1)}) custom-call(bf16[4,128,8,128]{3,2,1,0:T(8,128)(2,1)} %bitcast.14, bf16[4,128,16,128]{3,2,1,0:T(8,128)(2,1)} %bitcast.11, f32[2,10,128,128]{3,2,1,0:T(8,128)} %child_pivots.1, ...), custom_call_target="tpu_custom_call" | custom-call | flops 10000000000 | bytes 10000000 | tf_op jit(solution)/shard_map/pallas_call | solution.py:715
  73.3 0.0 copy-done.4
  73.3 0.0 copy-start
  73.3 1.3 %copy-done = bf16[512,1280]{1,0:T(8,128)(2,1)S(1)} copy-done((bf16[512,1280]{1,0:T(8,128)(2,1)S(1)}, bf16[512,1280]{1,0:T(8,128)(2,1)}, u32[]{:S(2)}) %copy-start) | copy-done | bytes 1310744
  74.6 0.0 copy-start.1
  74.6 1.0 %copy-done.1 = bf16[512,512]{1,0:T(8,128)(2,1)S(1)} copy-done((bf16[512,512]{1,0:T(8,128)(2,1)S(1)}, bf16[512,512]{1,0:T(8,128)(2,1)}, u32[]{:S(2)}) %copy-start.1) | copy-done | bytes 524312
  75.7 0.0 copy-start.2
  75.7 1.0 %copy-done.2 = bf16[2,128,896]{2,1,0:T(8,128)(2,1)S(1)} copy-done((bf16[2,128,896]{2,1,0:T(8,128)(2,1)S(1)}, bf16[2,128,896]{2,1,0:T(8,128)(2,1)}, u32[]{:S(2)}) %copy-start.2) | copy-done | bytes 458776
  76.7 0.0 copy-start.3
  76.7 1.0 %copy-done.3 = bf16[2,128,896]{2,1,0:T(8,128)(2,1)S(1)} copy-done((bf16[2,128,896]{2,1,0:T(8,128)(2,1)S(1)}, bf16[2,128,896]{2,1,0:T(8,128)(2,1)}, u32[]{:S(2)}) %copy-start.3) | copy-done | bytes 458776
  77.7 6.9 %shard_map.77 = (bf16[4,128,16,128]{3,2,1,0:T(8,128)(2,1)}, bf16[512,1280]{1,0:T(8,128)(2,1)}, bf16[512,512]{1,0:T(8,128)(2,1)}) custom-call(s32[2,54]{1,0:T(2,128)S(1)} %copy-done.4, f32[8192,128]{1,0:T(8,128)} %get-tuple-element.11.rest, bf16[2,128,896]{2,1,0:T(8,128)(2,1)S(1)} %copy-done.2, bf16[2,128,896]{2,1,0:T(8,128)(2,1)S(1)} %copy-done.3, ...), custom_call_target="tpu_custom_call" | custom-call | tf_op jit(solution)/shard_map/pallas_call | solution.py:804
Async XLA Ops:
  0.6 72.7 %copy-start.4 = (s32[2,54]{1,0:T(2,128)S(1)}, s32[2,54]{1,0:T(2,128)}, u32[]{:S(2)}) copy-start(s32[2,54]{1,0:T(2,128)} %maps.1) | copy-start | bytes 1300
  73.3 1.3 %copy-start = (bf16[512,1280]{1,0:T(8,128)(2,1)S(1)}, bf16[512,1280]{1,0:T(8,128)(2,1)}, u32[]{:S(2)}) copy-start(bf16[512,1280]{1,0:T(8,128)(2,1)} %get-tuple-element.14.panels) | copy-start | bytes 3932164
  74.6 1.0 %copy-start.1 = (bf16[512,512]{1,0:T(8,128)(2,1)S(1)}, bf16[512,512]{1,0:T(8,128)(2,1)}, u32[]{:S(2)}) copy-start(bf16[512,512]{1,0:T(8,128)(2,1)} %get-tuple-element.15.root_panels) | copy-start | bytes 1572868
  75.7 1.0 %copy-start.2 = (bf16[2,128,896]{2,1,0:T(8,128)(2,1)S(1)}, bf16[2,128,896]{2,1,0:T(8,128)(2,1)}, u32[]{:S(2)}) copy-start(bf16[2,128,896]{2,1,0:T(8,128)(2,1)} %get-tuple-element.12.keep) | copy-start | bytes 1376260
  76.7 1.0 %copy-start.3 = (bf16[2,128,896]{2,1,0:T(8,128)(2,1)S(1)}, bf16[2,128,896]{2,1,0:T(8,128)(2,1)}, u32[]{:S(2)}) copy-start(bf16[2,128,896]{2,1,0:T(8,128)(2,1)} %get-tuple-element.13.came) | copy-start | bytes 1376260

commit v4 on v3

--- a/solution.py
+++ b/solution.py
@@ -491,10 +491,10 @@
 
 def main_kernel(
     fronts, roots, child_pivots, root_pivots,
-    panels_out, root_panels_out, rest_out, keep_out, came_out,
-    craw, rraw, cwide, rwide, cpiv, rpiv,
+    panels_out, xown, rest, keep_out, came_out,
+    craw, rraw, cwide, rwide, ctile, rtile, cpiv, rpiv,
     top, down, side, rtop, rdown, rside,
-    hand, rhand, ctop, cown, cside, cother, xtop, xown, xside, xother, update,
+    hand, rhand, ctop, cown, cside, cother, xtop, xside, xother, update,
     load_sem, store_sem, tl_send, tl_recv, rtl_send, rtl_recv, line_send, line_recv, rline_send, rline_recv,
     t_send, t_recv, s_send, s_recv, rt_send, rt_recv, rs_send, rs_recv, u_send, u_recv,
     q_send, q_recv, rq_send, rq_recv,
@@ -526,57 +526,65 @@
     root_side_spread = PlaneShare(traffic, rside, rhand, rs_recv, rs_send)
     always = col >= 0
 
-    loads[0].wait()
-    for t in range(4):
-        cwide[t * 8 * B:(t + 1) * 8 * B, :] = craw[t].astype(F32).reshape(8 * B, B)
-
     order = [1 - child, 3 - child, child, 2 + child]
-
-    def place_column(line_buffer, count, line_top, wide, stride, order):
+    own_first = 1 + 3 * half
+    other_first = 5 - 4 * half
+
+    def part_tiles(raw, wide, tiles, t):
+        stride = raw.shape[2]
+        for b in range(0, B, 32):
+            at = b * stride
+            wide[at:at + 32 * stride, :] = raw[t, b:b + 32].astype(F32).reshape(32 * stride, B)
+        for s in range(stride):
+            tiles[s, t] = wide[pl.ds(s, B, stride=stride), :].astype(BF)
+
+    def place_top(line_top, tiles):
+        for extra, cond, index, place in line_top.held():
+            @pl.when(cond)
+            def _():
+                line_top.buffer[line_top.mine, place] = tiles[extra, 0]
+
+    def place_columns(line_buffer, count, line_top, tiles, order):
         for extra, cond, index, place in line_top.held():
             @pl.when((col + 8 * extra) < count)
             def _():
                 for n, t in enumerate(order):
-                    column = wide[pl.ds(t * B * stride + extra, B, stride=stride), :]
-                    line_buffer[index, n * B:(n + 1) * B] = column.astype(BF)
-
-                @pl.when(cond)
-                def _():
-                    line_top.buffer[line_top.mine, place] = wide[pl.ds(extra, B, stride=stride), :].astype(BF)
-
-    place_column(down, KC, top_line, cwide, 8, order)
-    own_first = 1 + 3 * half
-    other_first = 5 - 4 * half
+                    line_buffer[index, n * B:(n + 1) * B] = tiles[extra, t]
+
+    loads[0].wait()
+    part_tiles(craw, cwide.at[0], ctile, 0)
+    place_top(top_line, ctile)
+    pl.semaphore_wait(barrier, count)
+    top_line.begin()
+    for t in range(1, 4):
+        part_tiles(craw, cwide.at[t], ctile, t)
+    place_columns(down, KC, top_line, ctile, order)
+    line.begin()
 
     @pl.when(owns)
     def _():
         for s in range(4):
             columns = slice(s * B, (s + 1) * B)
-            side[mine % KC, :, columns] = cwide[pl.ds(own_first + s, B, stride=8), :].astype(BF)
-            hand[:, columns] = cwide[pl.ds(4 - 3 * half + s, B, stride=8), :].astype(BF)
-
-    pl.semaphore_wait(barrier, count)
-    top_line.begin()
-    line.begin()
-    side_spread.begin()
+            side[mine % KC, :, columns] = ctile[own_first + s, 0]
+            hand[:, columns] = ctile[4 - 3 * half + s, 0]
 
     loads[2].wait()
     for t in range(4):
-        for b in range(0, B, 32):
-            at = (t * B + b) * RS
-            rwide[at:at + 32 * RS, :] = rraw[t, b:b + 32].astype(F32).reshape(32 * RS, B)
-    place_column(rdown, KR, root_top_line, rwide, RS, range(4))
+        part_tiles(rraw, rwide.at[t], rtile, t)
+    place_top(root_top_line, rtile)
+    place_columns(rdown, KR, root_top_line, rtile, range(4))
 
     @pl.when(root_owns)
     def _():
         for s in range(8):
             columns = slice(s * B, (s + 1) * B)
-            rside[row % KR, :, columns] = rwide[pl.ds(s, B, stride=RS), :].astype(BF)
-            rhand[:, columns] = rwide[pl.ds(8 + s, B, stride=RS), :].astype(BF)
+            rside[row % KR, :, columns] = rtile[s, 0]
+            rhand[:, columns] = rtile[8 + s, 0]
 
     root_top_line.begin()
     top_line.finish()
     top_spread.begin()
+    side_spread.begin()
     line.relay(1)
     top_spread.relay()
     side_spread.relay()
@@ -624,14 +632,14 @@
     def update_own(n):
         product = dot_nn(cown[n * B:(n + 1) * B, :], cside[...])
         for s in range(4):
-            value = cwide[pl.ds(order[n] * 8 * B + own_first + s, B, stride=8), :]
+            value = ctile[own_first + s, order[n]].astype(F32)
             update[n, :, s * B:(s + 1) * B] = (value - product[:, s * B:(s + 1) * B]).astype(BF)
 
     def update_other(n):
         columns = pl.ds(pl.multiple_of((1 - half) * B, B), 3 * B)
         product = dot_nn(cown[n * B:(n + 1) * B, :], cother[:, columns])
         for s in range(3):
-            value = cwide[pl.ds(order[n] * 8 * B + other_first + s, B, stride=8), :]
+            value = ctile[other_first + s, order[n]].astype(F32)
             update[n, :, (4 + s) * B:(5 + s) * B] = (value - product[:, s * B:(s + 1) * B]).astype(BF)
 
     def send_update(n, part):
@@ -686,26 +694,19 @@
     root_line.finish()
     for pair in range(KR // 2):
         factor_own(pair, rdown, rpiv, xtop, xown, root_class, slice(0, 4 * B), 0)
-    root_panels_store = pltpu.make_async_copy(xown, root_panels_out, store_sem.at[3])
-    root_panels_store.start()
     for pair in range(KR // 2):
         from_sibling(xother, pair, rq_recv)
-    rest_stores = []
     for t in range(4):
         for buffer, first in ((xside, 8 * half), (xother, 8 - 8 * half)):
             product = dot_nn(xown[t * B:(t + 1) * B, :], buffer[...])
             for s in range(8):
-                place = pl.ds(t * RS * B + first + s, B, stride=RS)
-                rwide[place, :] = rwide[place, :] - product[:, s * B:(s + 1) * B]
-        block = pl.ds(t * RS * B, RS * B)
-        rest_stores.append(pltpu.make_async_copy(rwide.at[block], rest_out.at[block], store_sem.at[4 + t]))
-        rest_stores[-1].start()
+                rest[t, first + s] = rtile[first + s, t].astype(F32) - product[:, s * B:(s + 1) * B]
 
     for n in range(2):
         Starter().landed(came_out.at[n, :, pl.ds(0, 4 * B)], u_recv.at[0, n])
         Starter().landed(came_out.at[n, :, pl.ds(4 * B, 3 * B)], u_recv.at[1, n])
     traffic.drain()
-    for store in [keep_store, root_panels_store] + panels_stores + rest_stores:
+    for store in [keep_store] + panels_stores:
         store.wait()
 
 
@@ -715,19 +716,21 @@
     return pl.pallas_call(
         main_kernel,
         out_shape=[
-            jax.ShapeDtypeStruct((4 * B, KC * B), BF),
-            jax.ShapeDtypeStruct((4 * B, KR * B), BF),
-            jax.ShapeDtypeStruct((4 * B * RS, B), F32),
-            jax.ShapeDtypeStruct((2, B, CS * B), BF),
-            jax.ShapeDtypeStruct((2, B, CS * B), BF),
+            pltpu.VMEM((4 * B, KC * B), BF),
+            pltpu.VMEM((4 * B, KR * B), BF),
+            pltpu.VMEM((4, RS, B, B), F32),
+            pltpu.VMEM((2, B, CS * B), BF),
+            pltpu.VMEM((2, B, CS * B), BF),
         ],
         in_specs=[anywhere] * 4,
-        out_specs=[anywhere] * 5,
+        out_specs=[pl.BlockSpec(memory_space=pltpu.VMEM)] * 5,
         scratch_shapes=[
             pltpu.VMEM((4, B, 8, B), BF),
             pltpu.VMEM((4, B, RS, B), BF),
-            pltpu.VMEM((4 * B * 8, B), F32),
-            pltpu.VMEM((4 * B * RS, B), F32),
+            pltpu.VMEM((4, B * 8, B), F32),
+            pltpu.VMEM((4, B * RS, B), F32),
+            pltpu.VMEM((8, 4, B, B), BF),
+            pltpu.VMEM((RS, 4, B, B), BF),
             pltpu.VMEM((KC, B, B), F32),
             pltpu.VMEM((KR, B, B), F32),
             pltpu.VMEM((KC, KC // 2 + 1, B, B), BF),
@@ -743,7 +746,6 @@
             pltpu.VMEM((KC * B, 4 * B), BF),
             pltpu.VMEM((KC * B, 4 * B), BF),
             pltpu.VMEM((KR * B, KR * B), BF),
-            pltpu.VMEM((4 * B, KR * B), BF),
             pltpu.VMEM((KR * B, 8 * B), BF),
             pltpu.VMEM((KR * B, 8 * B), BF),
             pltpu.VMEM((4, B, CS * B), BF),
@@ -761,21 +763,17 @@
     )(fronts, roots, child_pivots, root_pivots)
 
 
-def add_kernel(maps, rest, keep, came, panels, root_panels, out, panels_out, root_panels_out, total, tiles, done, sems):
+def add_kernel(maps, rest, keep, came, panels, root_panels, out, panels_out, root_panels_out, total, wide, done, sems):
     child, half, row, col = position()
     passes = [
         pltpu.make_async_copy(panels, panels_out, sems.at[0]),
         pltpu.make_async_copy(root_panels, root_panels_out, sems.at[1]),
     ]
-    fetch = [pltpu.make_async_copy(source, tiles.at[n], sems.at[2 + n]) for n, source in enumerate((keep, came))]
-    height = RS * B
-    blocks = [pl.ds(t * height, height) for t in range(4)]
-    fetch += [pltpu.make_async_copy(rest.at[blocks[t]], total.at[blocks[t]], sems.at[4 + t]) for t in range(4)]
-    for copy in fetch + passes:
+    for copy in passes:
         copy.start()
-    for copy in fetch:
-        copy.wait()
-    for number, source in enumerate((child, 1 - child)):
+    for t in range(4):
+        total[t] = rest[t]
+    for source, tiles in ((child, keep), (1 - child, came)):
         for p in range(2):
             i = (2 * p + child) * 16 + half * 8 + row - KC
             for n in range(7):
@@ -786,14 +784,15 @@
                 def _():
                     below = maps[source, jnp.maximum(i, 0)] // 32
                     across = maps[source, jnp.maximum(j, 0)] // 8
-                    place = pl.ds(below * height + across, B, stride=RS)
-                    total[place, :] = total[place, :] + tiles[number, p, :, n * B:(n + 1) * B].astype(F32)
+                    tile = tiles[p, :, n * B:(n + 1) * B].astype(F32)
+                    total[below, across] = total[below, across] + tile
     stores = []
     for t in range(4):
+        for s in range(RS):
+            wide[t, pl.ds(s, B, stride=RS), :] = total[t, s]
         for b in range(0, B, 32):
-            at = (t * B + b) * RS
-            done[t, b:b + 32] = total[at:at + 32 * RS, :].astype(BF).reshape(32, RS, B)
-        stores.append(pltpu.make_async_copy(done.at[t], out.at[t], sems.at[8 + t]))
+            done[t, b:b + 32] = wide[t, b * RS:(b + 32) * RS, :].astype(BF).reshape(32, RS, B)
+        stores.append(pltpu.make_async_copy(done.at[t], out.at[t], sems.at[2 + t]))
         stores[-1].start()
     for copy in stores + passes:
         copy.wait()
@@ -808,15 +807,15 @@
             jax.ShapeDtypeStruct((4 * B, KC * B), BF),
             jax.ShapeDtypeStruct((4 * B, KR * B), BF),
         ],
-        in_specs=[pl.BlockSpec(memory_space=pltpu.SMEM)] + [anywhere] * 5,
+        in_specs=[pl.BlockSpec(memory_space=pltpu.SMEM)] + [pl.BlockSpec(memory_space=pltpu.VMEM)] * 5,
         out_specs=[anywhere] * 3,
         scratch_shapes=[
-            pltpu.VMEM((4 * B * RS, B), F32),
-            pltpu.VMEM((2, 2, B, CS * B), BF),
+            pltpu.VMEM((4, RS, B, B), F32),
+            pltpu.VMEM((4, B * RS, B), F32),
             pltpu.VMEM((4, B, RS, B), BF),
-            pltpu.SemaphoreType.DMA((12,)),
+            pltpu.SemaphoreType.DMA((6,)),
         ],
-        compiler_params=pltpu.CompilerParams(vmem_limit_bytes=48 * 2**20),
+        compiler_params=pltpu.CompilerParams(vmem_limit_bytes=24 * 2**20),
     )(maps, rest, keep, came, panels, root_panels)
 
 

time: 85 us -> 78 us (0.918)
  the two profiles are of different devices: /device:TPU:25 before, /device:TPU:34 now
where the time goes in v4:
time: 78 us; the launch traced here: 77.9 us
  Pallas kernels  77 us (99%)
  between operations  0.84 us (1%)
    pallas_call x1, Pallas kernels, main_step(): pl.pallas_call(main_kernel, out_shape=[pltpu.VMEM((4 * B, KC * B), BF), p...  72.5 us
    pallas_call x1, Pallas kernels, add_step(): pl.pallas_call(add_kernel, out_shape=[jax.ShapeDtypeStruct((4, B, RS, B),...  4.53 us

profile of v4, /device:TPU:34, one launch (start us, length us, event | category | flops | bytes accessed | tf_op | source)
XLA Modules:
  0.0 77.9 jit_solution(12825127736034861657)
XLA Ops:
  0.6 0.0 copy-start
  0.6 72.5 %shard_map.76 = (bf16[512,1280]{1,0:T(8,128)(2,1)S(1)}, bf16[512,512]{1,0:T(8,128)(2,1)S(1)}, f32[4,16,128,128]{3,2,1,0:T(8,128)S(1)}, bf16[2,128,896]{2,1,0:T(8,128)(2,1)S(1)}, bf16[2,128,896]{2,1,0:T(8,128)(2,1)S(1)}) custom-call(bf16[4,128,8,128]{3,2,1,0:T(8,128)(2,1)} %bitcast.14, bf16[4,128,16,128]{3,2,1,0:T(8,128)(2,1)} %bitcast.11, ...), custom_call_target="tpu_custom_call" | custom-call | flops 10000000000 | bytes 10000000 | tf_op jit(solution)/shard_map/pallas_call | solution.py:716
  73.2 0.0 copy-done
  73.2 4.5 %shard_map.77 = (bf16[4,128,16,128]{3,2,1,0:T(8,128)(2,1)}, bf16[512,1280]{1,0:T(8,128)(2,1)}, bf16[512,512]{1,0:T(8,128)(2,1)}) custom-call(s32[2,54]{1,0:T(2,128)S(1)} %copy-done, f32[4,16,128,128]{3,2,1,0:T(8,128)S(1)} %get-tuple-element.11.rest, bf16[2,128,896]{2,1,0:T(8,128)(2,1)S(1)} %get-tuple-element.12.keep, ...), custom_call_target="tpu_custom_call" | custom-call | tf_op jit(solution)/shard_map/pallas_call | solution.py:803
Async XLA Ops:
  0.6 72.5 %copy-start = (s32[2,54]{1,0:T(2,128)S(1)}, s32[2,54]{1,0:T(2,128)}, u32[]{:S(2)}) copy-start(s32[2,54]{1,0:T(2,128)} %maps.1) | copy-start | bytes 1300

commit v5 on v4

--- a/solution.py
+++ b/solution.py
@@ -568,6 +568,7 @@
             side[mine % KC, :, columns] = ctile[own_first + s, 0]
             hand[:, columns] = ctile[4 - 3 * half + s, 0]
 
+    side_spread.begin()
     loads[2].wait()
     for t in range(4):
         part_tiles(rraw, rwide.at[t], rtile, t)
@@ -584,7 +585,6 @@
     root_top_line.begin()
     top_line.finish()
     top_spread.begin()
-    side_spread.begin()
     line.relay(1)
     top_spread.relay()
     side_spread.relay()
@@ -702,10 +702,10 @@
             for s in range(8):
                 rest[t, first + s] = rtile[first + s, t].astype(F32) - product[:, s * B:(s + 1) * B]
 
+    traffic.drain()
     for n in range(2):
         Starter().landed(came_out.at[n, :, pl.ds(0, 4 * B)], u_recv.at[0, n])
         Starter().landed(came_out.at[n, :, pl.ds(4 * B, 3 * B)], u_recv.at[1, n])
-    traffic.drain()
     for store in [keep_store] + panels_stores:
         store.wait()
 

time: 78 us -> 75.4 us (0.967)
  the two profiles are of different devices: /device:TPU:34 before, /device:TPU:25 now
where the time goes in v5:
time: 75.4 us; the launch traced here: 74 us
  Pallas kernels  73.2 us (97%)
  between operations  0.84 us (1%)
    pallas_call x1, Pallas kernels, main_step(): pl.pallas_call(main_kernel, out_shape=[pltpu.VMEM((4 * B, KC * B), BF), p...  68.4 us
    pallas_call x1, Pallas kernels, add_step(): pl.pallas_call(add_kernel, out_shape=[jax.ShapeDtypeStruct((4, B, RS, B),...  4.8 us

profile of v5, /device:TPU:25, one launch (start us, length us, event | category | flops | bytes accessed | tf_op | source)
XLA Modules:
  0.0 74.0 jit_solution(5689561061876604511)
XLA Ops:
  0.6 0.0 copy-start
  0.6 68.4 %shard_map.76 = (bf16[512,1280]{1,0:T(8,128)(2,1)S(1)}, bf16[512,512]{1,0:T(8,128)(2,1)S(1)}, f32[4,16,128,128]{3,2,1,0:T(8,128)S(1)}, bf16[2,128,896]{2,1,0:T(8,128)(2,1)S(1)}, bf16[2,128,896]{2,1,0:T(8,128)(2,1)S(1)}) custom-call(bf16[4,128,8,128]{3,2,1,0:T(8,128)(2,1)} %bitcast.14, bf16[4,128,16,128]{3,2,1,0:T(8,128)(2,1)} %bitcast.11, ...), custom_call_target="tpu_custom_call" | custom-call | flops 10000000000 | bytes 10000000 | tf_op jit(solution)/shard_map/pallas_call | solution.py:716
  69.1 0.0 copy-done
  69.1 4.8 %shard_map.77 = (bf16[4,128,16,128]{3,2,1,0:T(8,128)(2,1)}, bf16[512,1280]{1,0:T(8,128)(2,1)}, bf16[512,512]{1,0:T(8,128)(2,1)}) custom-call(s32[2,54]{1,0:T(2,128)S(1)} %copy-done, f32[4,16,128,128]{3,2,1,0:T(8,128)S(1)} %get-tuple-element.11.rest, bf16[2,128,896]{2,1,0:T(8,128)(2,1)S(1)} %get-tuple-element.12.keep, ...), custom_call_target="tpu_custom_call" | custom-call | tf_op jit(solution)/shard_map/pallas_call | solution.py:803
Async XLA Ops:
  0.6 68.4 %copy-start = (s32[2,54]{1,0:T(2,128)S(1)}, s32[2,54]{1,0:T(2,128)}, u32[]{:S(2)}) copy-start(s32[2,54]{1,0:T(2,128)} %maps.1) | copy-start | bytes 1300
